TPU v7x, 32 devices: a whole 2x2x4 slice. The times are simulated.
32 devices in a mesh: head: 8 (over y, x, core), seq: 4 (over z).
Axes of the slice: x: 2, y: 2, z: 4, core: 2. Of those that a mesh axis runs over, the one named last changes fastest.
Arguments:
- tokens: bfloat16 [4096, 2048], P(('head', 'seq')), may hold values from -6 to 6
- keys: bfloat16 [4096, 2048], P(('head', 'seq')), may hold values from -6 to 6
- values: bfloat16 [4096, 2048], P(('head', 'seq')), may hold values from -6 to 6
- q_weight: bfloat16 [2048, 2048], P(('head', 'seq')), may hold values from -0.125 to 0.125
- o_weight: bfloat16 [2048, 2048], P(('head', 'seq')), may hold values from -0.75 to 0.75
- gate_weight: bfloat16 [2048, 5504], P(('head', 'seq')), may hold values from -0.125 to 0.125
- up_weight: bfloat16 [2048, 5504], P(('head', 'seq')), may hold values from -0.125 to 0.125
- down_weight: bfloat16 [5504, 2048], P(None, ('head', 'seq')), may hold values from -0.078125 to 0.078125
- attn_gain: bfloat16 [2048], P(('head', 'seq')), may hold values from 0.099609375 to 1.8984375
- ffn_gain: bfloat16 [2048], P(('head', 'seq')), may hold values from 0.099609375 to 1.8984375
- span_order: int32 [4, 16], P('seq'), may hold values from 0 to 15, as said below
- doc_lengths: int32 [4, 4], P('seq'), may hold values from 1 to 512, 1024 in all within a row
- cotangent: bfloat16 [4096, 2048], P(('head', 'seq')), may hold values from -6 to 6
Outputs:
- mixed_out: bfloat16 [4096, 2048], P(('head', 'seq'))
- d_tokens: bfloat16 [4096, 2048], P(('head', 'seq'))
- d_keys: bfloat16 [4096, 2048], P(('head', 'seq'))
- d_values: bfloat16 [4096, 2048], P(('head', 'seq'))
- d_q_weight: float32 [2048, 2048], P(('head', 'seq'))
- d_o_weight: float32 [2048, 2048], P(('head', 'seq'))
- d_gate_weight: float32 [2048, 5504], P(('head', 'seq'))
- d_up_weight: float32 [2048, 5504], P(('head', 'seq'))
- d_down_weight: float32 [5504, 2048], P(None, ('head', 'seq'))
- d_attn_gain: float32 [2048], P(('head', 'seq'))
- d_ffn_gain: float32 [2048], P(('head', 'seq'))
Inputs may be any that keep to these rules, and one draw needn't show every extreme that they name: Each row is a permutation of the span numbers; a device holds spans span_order[s, 2 h] and span_order[s, 2 h + 1] of its group. `doc_lengths`: each row sums to 1024; its largest entry is 512.
All inputs are finite; a program needn't handle non-finite values.
Results may differ from a plain program's by a relative error of at most 0.013.
Values may be sent and summed in bfloat16 or wider, within the bound.
A program may use at most 320 MiB of HBM per device.

v0:
```python
import math

import jax
import jax.numpy as jnp
from jax import lax
from jax.sharding import PartitionSpec as P

HEADS = 16


EPS = 1e-06


def rms_scale(field):
    return lax.rsqrt(jnp.mean(field * field, axis=-1, keepdims=True) + EPS)


def contract_rows(left, right):
    return lax.dot_general(
        left, right, (((0,), (0,)), ((), ())), preferred_element_type=jnp.float32
    )


def contract_cols(left, right):
    return lax.dot_general(
        left, right, (((1,), (1,)), ((), ())), preferred_element_type=jnp.float32
    )


def places(order_row, length_row, group):
    count = order_row.shape[0]
    width = group // count
    slots = jnp.arange(group, dtype=jnp.int32)
    which = slots // width
    picked = jnp.where(
        which[:, None] == jnp.arange(count, dtype=jnp.int32)[None, :], order_row[None, :], 0
    )
    seq_span = jnp.sum(picked, axis=1)
    position = seq_span * width + slots % width
    bounds = jnp.cumsum(length_row)
    segment = jnp.sum((position[:, None] >= bounds[None, :]).astype(jnp.int32), axis=1)
    return (position, segment)


def mask_rows(position, segment, start, rows):
    query_place = lax.dynamic_slice_in_dim(position, start, rows, 0)
    query_segment = lax.dynamic_slice_in_dim(segment, start, rows, 0)
    return (segment[None, :] == query_segment[:, None]) & (
        position[None, :] <= query_place[:, None]
    )


def attend(query, key_rows, value_rows, position, segment):
    group = query.shape[0]
    rows = math.gcd(group, 512)
    scale = 1.0 / math.sqrt(query.shape[-1])

    def block(start):
        query_rows = lax.dynamic_slice_in_dim(query, start, rows, 0)
        allowed = mask_rows(position, segment, start, rows)
        raw = jnp.einsum("qhd,khd->hqk", query_rows, key_rows, preferred_element_type=jnp.float32)
        logits = jnp.where(allowed[None], raw * scale, -1e30)
        top = jnp.max(logits, axis=-1, keepdims=True)
        expo = jnp.exp(logits - top)
        total = jnp.sum(expo, axis=-1, keepdims=True)
        probs = expo / total
        out_rows = jnp.einsum(
            "hqk,khd->qhd",
            probs.astype(jnp.bfloat16),
            value_rows,
            preferred_element_type=jnp.float32,
        )
        return (out_rows, (top + jnp.log(total))[..., 0])

    starts = jnp.arange(group // rows, dtype=jnp.int32) * rows
    out_blocks, log_totals = lax.map(block, starts)
    return (out_blocks.reshape(query.shape), log_totals)


def attend_back(query, key_rows, value_rows, grad_out, log_totals, position, segment):
    group = query.shape[0]
    rows = math.gcd(group, 512)
    scale = 1.0 / math.sqrt(query.shape[-1])

    def block(carry, inputs):
        key_sum, value_sum = carry
        start, log_total = inputs
        query_rows = lax.dynamic_slice_in_dim(query, start, rows, 0)
        grad_rows = lax.dynamic_slice_in_dim(grad_out, start, rows, 0)
        allowed = mask_rows(position, segment, start, rows)
        raw = jnp.einsum("qhd,khd->hqk", query_rows, key_rows, preferred_element_type=jnp.float32)
        logits = jnp.where(allowed[None], raw * scale, -1e30)
        probs = jnp.exp(logits - log_total[..., None])
        grad_probs = jnp.einsum(
            "qhd,khd->hqk", grad_rows, value_rows, preferred_element_type=jnp.float32
        )
        grad_logits = probs * (grad_probs - jnp.sum(probs * grad_probs, axis=-1, keepdims=True))
        grad_raw = (grad_logits * scale).astype(jnp.bfloat16)
        grad_query = jnp.einsum(
            "hqk,khd->qhd", grad_raw, key_rows, preferred_element_type=jnp.float32
        )
        key_sum = key_sum + jnp.einsum(
            "hqk,qhd->khd", grad_raw, query_rows, preferred_element_type=jnp.float32
        )
        value_sum = value_sum + jnp.einsum(
            "hqk,qhd->khd",
            probs.astype(jnp.bfloat16),
            grad_rows,
            preferred_element_type=jnp.float32,
        )
        return ((key_sum, value_sum), grad_query)

    starts = jnp.arange(group // rows, dtype=jnp.int32) * rows
    zeros = jnp.zeros(query.shape, jnp.float32)
    (key_sum, value_sum), grad_blocks = lax.scan(block, (zeros, zeros), (starts, log_totals))
    grad_query = grad_blocks.reshape(query.shape).astype(jnp.bfloat16)
    return (grad_query, key_sum.astype(jnp.bfloat16), value_sum.astype(jnp.bfloat16))


def per_device(
    tokens,
    keys,
    values,
    q_weight,
    o_weight,
    gate_weight,
    up_weight,
    down_weight,
    attn_gain,
    ffn_gain,
    span_order,
    doc_lengths,
    cotangent,
):
    full_q, full_o, full_gate, full_up, gain_one, gain_two = (
        lax.all_gather(q_weight, ("head", "seq"), axis=0, tiled=True),
        lax.all_gather(o_weight, ("head", "seq"), axis=0, tiled=True),
        lax.all_gather(gate_weight, ("head", "seq"), axis=0, tiled=True),
        lax.all_gather(up_weight, ("head", "seq"), axis=0, tiled=True),
        lax.all_gather(attn_gain, ("head", "seq"), axis=0, tiled=True),
        lax.all_gather(ffn_gain, ("head", "seq"), axis=0, tiled=True),
    )
    full_down = lax.all_gather(down_weight, ("head", "seq"), axis=1, tiled=True)
    gain_attn = gain_one.astype(jnp.float32)
    gain_ffn = gain_two.astype(jnp.float32)
    local_rows = tokens.shape[0]
    width = tokens.shape[1]
    shape3 = (local_rows, HEADS, width // HEADS)
    inputs = tokens.astype(jnp.float32)
    scale_one = rms_scale(inputs)
    normed_one = inputs * scale_one
    attn_in = (normed_one * gain_attn).astype(jnp.bfloat16)
    query = jnp.dot(attn_in, full_q, preferred_element_type=jnp.float32).astype(jnp.bfloat16)
    query_heads, key_heads, value_heads = (
        lax.all_to_all(query.reshape(shape3), "head", split_axis=1, concat_axis=0, tiled=True),
        lax.all_to_all(keys.reshape(shape3), "head", split_axis=1, concat_axis=0, tiled=True),
        lax.all_to_all(values.reshape(shape3), "head", split_axis=1, concat_axis=0, tiled=True),
    )
    group = query_heads.shape[0]
    position, segment = places(span_order[0], doc_lengths[0], group)
    out_heads, log_totals = attend(query_heads, key_heads, value_heads, position, segment)
    attended = lax.all_to_all(
        out_heads.astype(jnp.bfloat16), "head", split_axis=0, concat_axis=1, tiled=True
    ).reshape(local_rows, width)
    hidden = inputs + jnp.dot(attended, full_o, preferred_element_type=jnp.float32)
    scale_two = rms_scale(hidden)
    normed_two = hidden * scale_two
    ffn_in = (normed_two * gain_ffn).astype(jnp.bfloat16)
    gate = jnp.dot(ffn_in, full_gate, preferred_element_type=jnp.float32)
    up_part = jnp.dot(ffn_in, full_up, preferred_element_type=jnp.float32)
    act = (jax.nn.silu(gate) * up_part).astype(jnp.bfloat16)
    mixed_out = (hidden + jnp.dot(act, full_down, preferred_element_type=jnp.float32)).astype(
        jnp.bfloat16
    )
    grad_act = contract_cols(cotangent, full_down)
    sigma = jax.nn.sigmoid(gate)
    grad_gate = (grad_act * up_part * sigma * (1.0 + gate * (1.0 - sigma))).astype(jnp.bfloat16)
    grad_up = (grad_act * gate * sigma).astype(jnp.bfloat16)
    grad_ffn_in = contract_cols(grad_gate, full_gate) + contract_cols(grad_up, full_up)
    grad_gain_two = jnp.sum(grad_ffn_in * normed_two, axis=0)
    scaled_two = grad_ffn_in * gain_ffn
    grad_hidden = cotangent.astype(jnp.float32) + scale_two * (
        scaled_two - normed_two * jnp.mean(scaled_two * normed_two, axis=-1, keepdims=True)
    )
    grad_hidden_low = grad_hidden.astype(jnp.bfloat16)
    grad_attended = contract_cols(grad_hidden_low, full_o).astype(jnp.bfloat16)
    grad_out_heads = lax.all_to_all(
        grad_attended.reshape(shape3), "head", split_axis=1, concat_axis=0, tiled=True
    )
    grad_q_heads, grad_k_heads, grad_v_heads = attend_back(
        query_heads, key_heads, value_heads, grad_out_heads, log_totals, position, segment
    )
    grad_query, grad_keys, grad_values = (
        lax.all_to_all(grad_q_heads, "head", split_axis=0, concat_axis=1, tiled=True),
        lax.all_to_all(grad_k_heads, "head", split_axis=0, concat_axis=1, tiled=True),
        lax.all_to_all(grad_v_heads, "head", split_axis=0, concat_axis=1, tiled=True),
    )
    grad_query = grad_query.reshape(local_rows, width)
    grad_attn_in = contract_cols(grad_query, full_q)
    grad_gain_one = jnp.sum(grad_attn_in * normed_one, axis=0)
    scaled_one = grad_attn_in * gain_attn
    grad_tokens = grad_hidden + scale_one * (
        scaled_one - normed_one * jnp.mean(scaled_one * normed_one, axis=-1, keepdims=True)
    )
    q_term = contract_rows(attn_in, grad_query)
    o_term = contract_rows(attended, grad_hidden_low)
    gate_term = contract_rows(ffn_in, grad_gate)
    up_term = contract_rows(ffn_in, grad_up)
    down_term = contract_rows(act, cotangent)
    gain_terms = jnp.stack([grad_gain_one, grad_gain_two])
    grad_q_weight, grad_o_weight, grad_gate_weight, grad_up_weight = (
        lax.psum_scatter(q_term, ("head", "seq"), scatter_dimension=0, tiled=True),
        lax.psum_scatter(o_term, ("head", "seq"), scatter_dimension=0, tiled=True),
        lax.psum_scatter(gate_term, ("head", "seq"), scatter_dimension=0, tiled=True),
        lax.psum_scatter(up_term, ("head", "seq"), scatter_dimension=0, tiled=True),
    )
    down_sum, gain_sums = (
        lax.psum_scatter(down_term, ("head", "seq"), scatter_dimension=1, tiled=True),
        lax.psum_scatter(gain_terms, ("head", "seq"), scatter_dimension=1, tiled=True),
    )
    return (
        mixed_out,
        grad_tokens.astype(jnp.bfloat16),
        grad_keys.reshape(local_rows, width),
        grad_values.reshape(local_rows, width),
        grad_q_weight,
        grad_o_weight,
        grad_gate_weight,
        grad_up_weight,
        down_sum,
        gain_sums[0],
        gain_sums[1],
    )


def solution(mesh):
    placed = (
        P(("head", "seq"), None),
        P(("head", "seq"), None),
        P(("head", "seq"), None),
        P(("head", "seq"), None),
        P(("head", "seq"), None),
        P(("head", "seq"), None),
        P(("head", "seq"), None),
        P(None, ("head", "seq")),
        P(("head", "seq")),
        P(("head", "seq")),
        P("seq", None),
        P("seq", None),
        P(("head", "seq"), None),
    )
    return jax.shard_map(
        per_device,
        mesh=mesh,
        in_specs=placed,
        out_specs=(
            P(("head", "seq"), None),
            P(("head", "seq"), None),
            P(("head", "seq"), None),
            P(("head", "seq"), None),
            P(("head", "seq"), None),
            P(("head", "seq"), None),
            P(("head", "seq"), None),
            P(("head", "seq"), None),
            P(None, ("head", "seq")),
            P(("head", "seq")),
            P(("head", "seq")),
        ),
        check_vma=False,
    )
```

profile of v0, /device:TPU:0, one launch (start us, length us, event | category | flops | bytes accessed | tf_op | source)
XLA Modules:
  0.0 4496.1 jit_solution(8922970533278333038)
XLA Ops:
  12.6 5.2 all-to-all-start.1
  18.3 45.1 %all-reduce.2 = (bf16[2048]{0:T(1024)(128)(2,1)S(1)}, bf16[2048]{0:T(1024)(128)(2,1)S(1)}) all-reduce(bf16[2048]{0:T(1024)(128)(2,1)S(1)} %dynamic-update-slice, bf16[2048]{0:T(1024)(128)(2,1)S(1)} %dynamic-update-slice.1), channel_id=1, replica_groups=mesh['head'=8,'seq'=4] {'head','seq'}, use_global_device_ids=true, to_apply=%add | all-reduce | flops 4096 | bytes 16384
  64.7 3.6 all-to-all-start.2
  68.3 30.4 all-gather.6.cloned.1.call-done
  98.7 4.7 fusion.60
  104.3 3.5 all-to-all-start
  108.8 10.6 all-to-all-done
  119.5 14.6 while.27
  135.5 3.8 all-to-all-start.3
  139.2 9.7 all-to-all-done.3
  151.1 29.5 all-gather.8.cloned.1.call-done
  180.6 4.7 multiply_reduce_fusion.3
  185.6 138.6 %all-gather.10.cloned.1.call-done = bf16[2048,5504]{1,0:T(8,128)(2,1)} async-done(((bf16[64,5504]{1,0:T(8,128)(2,1)}), bf16[2048,5504]{1,0:T(8,128)(2,1)}) %all-gather.10.cloned.1.call-update) | async-done | bytes 22544400 | tf_op jit(solution)/shard_map/all_gather | solution.py:138
  324.1 12.2 fusion.85
  336.3 130.8 %all-gather.12.cloned.1.call-done = bf16[2048,5504]{1,0:T(8,128)(2,1)} async-done(((bf16[64,5504]{1,0:T(8,128)(2,1)}), bf16[2048,5504]{1,0:T(8,128)(2,1)}) %all-gather.12.cloned.1.call-update) | async-done | bytes 22544400 | tf_op jit(solution)/shard_map/all_gather | solution.py:139
  467.1 12.1 fusion.86
  479.2 130.8 %all-gather.14.cloned.1.call-done = bf16[5504,2048]{0,1:T(8,128)(2,1)} async-done(((bf16[5504,64]{0,1:T(8,128)(2,1)}), bf16[5504,2048]{0,1:T(8,128)(2,1)}) %all-gather.14.cloned.1.call-update) | async-done | bytes 22544400 | tf_op jit(solution)/shard_map/all_gather | solution.py:143
  610.0 14.4 multiply_convert_fusion.1
  624.4 23.6 fusion.87
  648.0 13.4 multiply_reduce_fusion.1
  663.0 6.7 fusion.61
  670.6 3.5 all-to-all-start.4
  674.2 9.6 all-to-all-done.4
  686.5 57.2 %while.28 = (s32[]{:T(128)}, f32[1024,2,128]{0,2,1:T(8,128)}, f32[1024,2,128]{0,2,1:T(8,128)S(1)}, bf16[2,512,2,128]{3,1,0,2:T(8,128)(2,1)}, s32[2]{0:T(128)S(1)...) while((s32[]{:T(128)}, f32[1024,2,128]{0,2,1:T(8,128)}, ...), condition=%wide.region_12.13_spmd.clone, body=%wide.region_10.12_spmd.clone.sunk | while | flops 1359482880 | bytes 54559456 | solution.py:115
  689.7 4.1 subtract_exponential_fusion.3
  696.5 8.0 fusion.157
  704.6 7.6 fusion.159
  712.2 2.8 fusion.158
  718.2 4.1 subtract_exponential_fusion.3
  725.0 8.3 fusion.157
  733.3 7.6 fusion.159
  745.4 12.2 all_to_all.132
  758.6 7.6 fusion.68
  767.7 8.1 fusion.70
  776.8 8.2 fusion.73
  786.0 18.8 fusion.88
  804.9 18.8 fusion.89
  824.8 18.8 fusion.90
  845.9 3.5 all-to-all-start.6
  850.7 8.6 all-to-all-done.6
  859.3 4.4 all-to-all-start.7
  863.7 12.6 fusion.55
  883.4 17.3 reduce-scatter.19.cloned.1.call-done
  902.8 361.6 %reduce-scatter.11.cloned.1.call-done = f32[64,2048]{1,0:T(8,128)} async-done(((f32[2048,2048]{1,0:T(8,128)}), f32[64,2048]{1,0:T(8,128)}) %reduce-scatter.11.cloned.1.call-update) | async-done | bytes 524304 | tf_op jit(solution)/shard_map/reduce_scatter | solution.py:213
  1264.4 365.2 %reduce-scatter.9.cloned.1.call-done = f32[64,2048]{1,0:T(8,128)} async-done(((f32[2048,2048]{1,0:T(8,128)}), f32[64,2048]{1,0:T(8,128)}) %reduce-scatter.9.cloned.1.call-update) | async-done | bytes 524304 | tf_op jit(solution)/shard_map/reduce_scatter | solution.py:212
  1629.6 951.6 %reduce-scatter.13.cloned.1.call-done = f32[64,5504]{1,0:T(8,128)} async-done(((f32[2048,5504]{1,0:T(8,128)}), f32[64,5504]{1,0:T(8,128)}) %reduce-scatter.13.cloned.1.call-update) | async-done | bytes 1409040 | tf_op jit(solution)/shard_map/reduce_scatter | solution.py:214
  2581.2 953.8 %reduce-scatter.15.cloned.1.call-done = f32[64,5504]{1,0:T(8,128)} async-done(((f32[2048,5504]{1,0:T(8,128)}), f32[64,5504]{1,0:T(8,128)}) %reduce-scatter.15.cloned.1.call-update) | async-done | bytes 1409040 | tf_op jit(solution)/shard_map/reduce_scatter | solution.py:215
  3535.1 954.0 %reduce-scatter.17.cloned.1.call-done = f32[5504,64]{0,1:T(8,128)} async-done(((f32[5504,2048]{0,1:T(8,128)}), f32[5504,64]{0,1:T(8,128)}) %reduce-scatter.17.cloned.1.call-update) | async-done | bytes 1409040 | tf_op jit(solution)/shard_map/reduce_scatter | solution.py:218
  (158 shorter events, 59.5 us)
Async XLA Ops:
  7.2 10.6 copy-start.24
  7.2 10.9 copy-start.25
  7.2 56.3 %copy-start.18 = (bf16[128,2048]{1,0:T(8,128)(2,1)S(1)}, bf16[128,2048]{1,0:T(8,128)(2,1)}, u32[]{:S(2)}) copy-start(bf16[128,2048]{1,0:T(8,128)(2,1)} %param.19) | copy-start | bytes 1572868
  7.2 57.3 %copy-start.2 = (bf16[128,2048]{1,0:T(8,128)(2,1)S(1)}, bf16[128,2048]{1,0:T(8,128)(2,1)}, u32[]{:S(2)}) copy-start(bf16[128,2048]{1,0:T(8,128)(2,1)} %param.17) | copy-start | bytes 1572868
  7.2 91.4 %all-gather.6.cloned.1.call-start = ((), (), s32[]{:S(2)}) async-start(), calls=%async_computation.14 | async-start | bytes 8650752 | tf_op jit(solution)/shard_map/all_gather | solution.py:136
  8.0 172.7 %all-gather.8.cloned.1.call-start = ((), (), s32[]{:S(2)}) async-start(), calls=%async_computation.15 | async-start | bytes 8650752 | tf_op jit(solution)/shard_map/all_gather | solution.py:137
  8.7 315.4 %all-gather.10.cloned.1.call-start = ((), (), s32[]{:S(2)}) async-start(), calls=%async_computation.16 | async-start | bytes 23248896 | tf_op jit(solution)/shard_map/all_gather | solution.py:138
  9.4 457.6 %all-gather.12.cloned.1.call-start = ((), (), s32[]{:S(2)}) async-start(), calls=%async_computation.17 | async-start | bytes 23248896 | tf_op jit(solution)/shard_map/all_gather | solution.py:139
  10.0 600.0 %all-gather.14.cloned.1.call-start = ((), (), s32[]{:S(2)}) async-start(), calls=%async_computation.18 | async-start | bytes 23248896 | tf_op jit(solution)/shard_map/all_gather | solution.py:143
  12.6 52.0 %all-to-all-start.1 = ((bf16[128,16,128]{0,2,1:T(8,128)(2,1)}), bf16[128,16,128]{0,2,1:T(8,128)(2,1)S(1)}, u32[]{:S(2)}, u32[]{:S(2)}) async-start(bf16[128,16,128]{0,2,1:T(8,128)(2,1)} %bitcast.10), calls=%async_computation.1 | async-start | bytes 1048576 | tf_op jit(solution)/shard_map/all_to_all | solution.py:156
  63.5 39.9 copy-start.19
  64.7 38.7 copy-start.21
  64.7 39.6 all-to-all-start.2
  68.3 39.6 copy-start.26
  68.3 39.8 copy-start.23
  104.3 15.1 all-to-all-start
  134.1 46.5 %copy-start.12 = (bf16[1024,2,128]{2,0,1:T(8,128)(2,1)}, bf16[1024,2,128]{2,0,1:T(8,128)(2,1)S(1)}, u32[]{:S(2)}) copy-start(bf16[1024,2,128]{2,0,1:T(8,128)(2,1)S(1)} %get-tuple-element.467) | copy-start | bytes 1572868
  135.5 13.4 all-to-all-start.3
  151.1 34.3 copy-start.10
  185.4 476.0 %copy-start = (f32[128,2048]{1,0:T(8,128)}, f32[128,2048]{1,0:T(8,128)S(1)}, u32[]{:S(2)}) copy-start(f32[128,2048]{1,0:T(8,128)S(1)} %get-tuple-element.223) | copy-start | bytes 3145732
  185.6 281.5 %copy-start.6 = (bf16[128,2048]{1,0:T(8,128)(2,1)}, bf16[128,2048]{1,0:T(8,128)(2,1)S(1)}, u32[]{:S(2)}) copy-start(bf16[128,2048]{1,0:T(8,128)(2,1)S(1)} %multiply_convert_fusion.4) | copy-start | bytes 1572868
  624.4 23.6 copy-start.8
  624.4 23.6 copy-start.9
  648.0 13.4 copy-start.15
  663.0 6.7 copy-start.3
  670.6 13.2 all-to-all-start.4
  674.1 226.6 %reduce-scatter.19.cloned.1.call-start = ((), (), s32[]{:S(2)}) async-start(), calls=%async_computation.24 | async-start | bytes 1081344
  683.8 0.8 copy-start.17
  743.8 14.9 copy-start.20
  743.8 14.9 copy-start.22
  758.6 9.0 copy-start.4
  758.6 9.0 copy-start.11
  767.6 496.8 %reduce-scatter.11.cloned.1.call-start = ((), (), s32[]{:S(2)}) async-start(), calls=%async_computation.20 | async-start | bytes 17301504 | tf_op jit(solution)/shard_map/reduce_scatter | solution.py:213
  775.7 1.0 copy-start.13
  775.8 853.8 %reduce-scatter.9.cloned.1.call-start = ((), (), s32[]{:S(2)}) async-start(), calls=%async_computation.19 | async-start | bytes 17301504 | tf_op jit(solution)/shard_map/reduce_scatter | solution.py:212
  785.0 1.0 copy-start.7
  785.0 1796.2 %reduce-scatter.13.cloned.1.call-start = ((), (), s32[]{:S(2)}) async-start(), calls=%async_computation.21 | async-start | bytes 46497792 | tf_op jit(solution)/shard_map/reduce_scatter | solution.py:214
  804.9 2730.2 %reduce-scatter.15.cloned.1.call-start = ((), (), s32[]{:S(2)}) async-start(), calls=%async_computation.22 | async-start | bytes 46497792 | tf_op jit(solution)/shard_map/reduce_scatter | solution.py:215
  823.7 1.0 copy-start.16
  823.8 3665.3 %reduce-scatter.17.cloned.1.call-start = ((), (), s32[]{:S(2)}) async-start(), calls=%async_computation.23 | async-start | bytes 46497792 | tf_op jit(solution)/shard_map/reduce_scatter | solution.py:218
  843.6 20.1 copy-start.1
  845.9 13.4 all-to-all-start.6
  859.3 20.4 all-to-all-start.7
  876.3 6.0 copy-start.5
  876.3 6.0 copy-start.14
Sparse Core Ops, SparseCore 0:
  11.0 87.6 all-gather.5
  101.6 78.9 all-gather.7
  183.5 140.6 all-gather.9
  326.8 140.2 all-gather.11
  469.8 140.2 all-gather.13
  767.7 132.9 reduce-scatter.18
  903.7 360.6 reduce-scatter.10
  1267.4 362.1 reduce-scatter.8
  1632.6 948.5 reduce-scatter.12
  2584.1 950.9 reduce-scatter.14
  3538.1 950.9 reduce-scatter.16
where the time goes:
time: 4500 us
  waiting for transfers between devices  4110 us (91%)
  matrix products  241 us (5%)
  blocking collectives  57.3 us (1%)
    reduce_scatter x1, waiting for transfers between devices, per_device(): lax.psum_scatter(down_term, ('head', 'seq'), scatter_dimension=1, tiled=T...  954 us
    reduce_scatter x1, waiting for transfers between devices, per_device(): lax.psum_scatter(up_term, ('head', 'seq'), scatter_dimension=0, tiled=True)  954 us
    reduce_scatter x1, waiting for transfers between devices, per_device(): lax.psum_scatter(gate_term, ('head', 'seq'), scatter_dimension=0, tiled=T...  952 us
    reduce_scatter x1, waiting for transfers between devices, per_device(): lax.psum_scatter(q_term, ('head', 'seq'), scatter_dimension=0, tiled=True)  365 us
    reduce_scatter x1, waiting for transfers between devices, per_device(): lax.psum_scatter(o_term, ('head', 'seq'), scatter_dimension=0, tiled=True)  362 us
    all_gather x1, waiting for transfers between devices, per_device(): lax.all_gather(gate_weight, ('head', 'seq'), axis=0, tiled=True)  139 us
    all_gather x1, waiting for transfers between devices, per_device(): full_down = lax.all_gather(down_weight, ('head', 'seq'), axis=1, tiled=True)  131 us
    all_gather x1, waiting for transfers between devices, per_device(): lax.all_gather(up_weight, ('head', 'seq'), axis=0, tiled=True)  131 us
  transfers between devices with their start and end apart: 18, of which 15 were waited for; matrix products, arithmetic and copies ran while one was open for 3% of the time, Pallas kernels for 0%

commit v1 on v0

v1 whole, which is shorter than its diff:
```python
import functools
import math

import jax
import jax.numpy as jnp
from jax import lax
from jax.experimental import pallas as pl
from jax.experimental.pallas import tpu as pltpu
from jax.sharding import PartitionSpec as P

HEAD_DIM = 128
EPS = 1e-06
BF16 = jnp.bfloat16
F32 = jnp.float32


def rms_scale(field):
    return lax.rsqrt(jnp.mean(field * field, axis=-1, keepdims=True) + EPS)


def dot(left, right, dims):
    return lax.dot_general(left, right, (dims, ((), ())), preferred_element_type=F32)


def places(order_row, length_row, group):
    count = order_row.shape[0]
    width = group // count
    slots = jnp.arange(group, dtype=jnp.int32)
    which = slots // width
    picked = jnp.where(
        which[:, None] == jnp.arange(count, dtype=jnp.int32)[None, :], order_row[None, :], 0
    )
    position = jnp.sum(picked, axis=1) * width + slots % width
    bounds = jnp.cumsum(length_row)
    segment = jnp.sum((position[:, None] >= bounds[None, :]).astype(jnp.int32), axis=1)
    return (position, segment)


def attend_kernel(q_ref, k_ref, v_ref, place_q, place_k, out_ref, lse_ref):
    scale = 1.0 / math.sqrt(HEAD_DIM)
    raw = dot(q_ref[...], k_ref[...], ((1,), (1,)))
    allowed = (place_q[:, 1:2] == place_k[1:2, :]) & (place_k[0:1, :] <= place_q[:, 0:1])
    logits = jnp.where(allowed, raw * scale, -1e30)
    top = jnp.max(logits, axis=-1, keepdims=True)
    expo = jnp.exp(logits - top)
    total = jnp.sum(expo, axis=-1, keepdims=True)
    probs = expo * (1.0 / total)
    out_ref[...] = dot(probs.astype(BF16), v_ref[...], ((1,), (0,))).astype(BF16)
    lse_ref[...] = jnp.broadcast_to(top + jnp.log(total), lse_ref.shape)


def attend(query, keys, values, place_q, place_k):
    group, width = query.shape
    heads = width // HEAD_DIM
    rows = min(group, 256)
    block = pl.BlockSpec((rows, HEAD_DIM), lambda h, i: (i, h))
    whole = pl.BlockSpec((group, HEAD_DIM), lambda h, i: (0, h))
    return pl.pallas_call(
        attend_kernel,
        grid=(heads, group // rows),
        in_specs=[
            block,
            whole,
            whole,
            pl.BlockSpec((rows, 2), lambda h, i: (i, 0)),
            pl.BlockSpec((2, group), lambda h, i: (0, 0)),
        ],
        out_specs=[block, block],
        out_shape=[
            jax.ShapeDtypeStruct((group, width), BF16),
            jax.ShapeDtypeStruct((group, width), F32),
        ],
        compiler_params=pltpu.CompilerParams(vmem_limit_bytes=48 << 20),
        cost_estimate=pl.CostEstimate(
            flops=4 * group * group * width,
            bytes_accessed=12 * group * width,
            transcendentals=heads * group * group,
        ),
        name="attend",
    )(query, keys, values, place_q, place_k)


def attend_back_kernel(
    q_ref, k_ref, v_ref, do_ref, lse_ref, place_q, place_k, dq_ref, dk_ref, dv_ref, dk_sum, dv_sum
):
    step = pl.program_id(1)
    scale = 1.0 / math.sqrt(HEAD_DIM)
    query, keys, grad = q_ref[...], k_ref[...], do_ref[...]
    raw = dot(query, keys, ((1,), (1,)))
    allowed = (place_q[:, 1:2] == place_k[1:2, :]) & (place_k[0:1, :] <= place_q[:, 0:1])
    logits = jnp.where(allowed, raw * scale, -1e30)
    probs = jnp.exp(logits - lse_ref[:, :1])
    grad_probs = dot(grad, v_ref[...], ((1,), (1,)))
    inner = jnp.sum(probs * grad_probs, axis=-1, keepdims=True)
    grad_raw = (probs * (grad_probs - inner) * scale).astype(BF16)
    dq_ref[...] = dot(grad_raw, keys, ((1,), (0,))).astype(BF16)

    @pl.when(step == 0)
    def _():
        dk_sum[...] = jnp.zeros_like(dk_sum)
        dv_sum[...] = jnp.zeros_like(dv_sum)

    dk_sum[...] += dot(grad_raw, query, ((0,), (0,)))
    dv_sum[...] += dot(probs.astype(BF16), grad, ((0,), (0,)))

    @pl.when(step == pl.num_programs(1) - 1)
    def _():
        dk_ref[...] = dk_sum[...].astype(BF16)
        dv_ref[...] = dv_sum[...].astype(BF16)


def attend_back(query, keys, values, grad, lse, place_q, place_k):
    group, width = query.shape
    heads = width // HEAD_DIM
    rows = min(group, 256)
    block = pl.BlockSpec((rows, HEAD_DIM), lambda h, i: (i, h))
    whole = pl.BlockSpec((group, HEAD_DIM), lambda h, i: (0, h))
    full = jax.ShapeDtypeStruct((group, width), BF16)
    return pl.pallas_call(
        attend_back_kernel,
        grid=(heads, group // rows),
        in_specs=[
            block,
            whole,
            whole,
            block,
            block,
            pl.BlockSpec((rows, 2), lambda h, i: (i, 0)),
            pl.BlockSpec((2, group), lambda h, i: (0, 0)),
        ],
        out_specs=[block, whole, whole],
        out_shape=[full, full, full],
        scratch_shapes=[pltpu.VMEM((group, HEAD_DIM), F32)] * 2,
        compiler_params=pltpu.CompilerParams(vmem_limit_bytes=48 << 20),
        cost_estimate=pl.CostEstimate(
            flops=10 * group * group * width,
            bytes_accessed=18 * group * width,
            transcendentals=heads * group * group,
        ),
        name="attend_back",
    )(query, keys, values, grad, lse, place_q, place_k)


def to_slices(weight, nh):
    rows, cols = weight.shape
    parts = weight.reshape(rows, nh, cols // nh).swapaxes(0, 1)
    return lax.all_to_all(parts, "head", 0, 0, tiled=False).reshape(nh * rows, cols // nh)


def from_slices(part, nh):
    rows, cols = part.shape
    parts = part.reshape(nh, rows // nh, cols)
    parts = lax.all_to_all(parts, "head", 0, 0, tiled=False)
    return parts.swapaxes(0, 1).reshape(rows // nh, nh * cols)


def gather_seq(part):
    return lax.all_gather(part, "seq", axis=0, tiled=True)


def scatter_seq(full):
    return lax.psum_scatter(full.astype(BF16), "seq", scatter_dimension=0, tiled=True)


def gather_head(part):
    return lax.all_gather(part, "head", axis=0, tiled=True)


def scatter_head(full):
    return lax.psum_scatter(full.astype(BF16), "head", scatter_dimension=0, tiled=True)


def per_device(
    nh,
    ns,
    tokens,
    keys,
    values,
    q_weight,
    o_weight,
    gate_weight,
    up_weight,
    down_weight,
    attn_gain,
    ffn_gain,
    span_order,
    doc_lengths,
    cotangent,
):
    local, width = tokens.shape
    rows = q_weight.shape[0]

    def shuffle(field):
        return field.reshape(local, nh, ns, rows).swapaxes(1, 2).reshape(local, width)

    def unshuffle(field):
        return field.reshape(local, ns, nh, rows).swapaxes(1, 2).reshape(local, width)

    gain_one = attn_gain.astype(F32)[:, None]
    gain_two = ffn_gain.astype(F32)[:, None]
    inputs = tokens.astype(F32)
    scale_one = rms_scale(inputs)
    normed_one = inputs * scale_one
    normed_one_all = gather_head(shuffle(normed_one.astype(BF16)))
    w_q = gather_seq(to_slices((q_weight * gain_one).astype(BF16), nh))
    key_heads = to_slices(keys, nh)
    value_heads = to_slices(values, nh)
    w_o = gather_seq(o_weight)
    w_gate = gather_seq(to_slices((gate_weight * gain_two).astype(BF16), nh))
    w_up = gather_seq(to_slices((up_weight * gain_two).astype(BF16), nh))
    w_down = gather_seq(to_slices(down_weight.T, nh))
    cotangent_all = gather_head(shuffle(cotangent))

    group = normed_one_all.shape[0]
    position, segment = places(span_order[0], doc_lengths[0], group)
    place_q = jnp.stack([position, segment], axis=1)
    place_k = jnp.stack([position, segment], axis=0)

    query = dot(normed_one_all, w_q, ((1,), (0,))).astype(BF16)
    attended, lse = attend(query, key_heads, value_heads, place_q, place_k)
    hidden = inputs + scatter_head(dot(attended, w_o, ((1,), (0,)))).astype(F32)
    scale_two = rms_scale(hidden)
    normed_two = hidden * scale_two
    normed_two_all = gather_head(shuffle(normed_two.astype(BF16)))

    gate = dot(normed_two_all, w_gate, ((1,), (0,)))
    up = dot(normed_two_all, w_up, ((1,), (0,)))
    sigma = jax.nn.sigmoid(gate)
    act = (gate * sigma * up).astype(BF16)
    down_sum = scatter_seq(dot(cotangent_all, act, ((0,), (0,))))
    grad_act = dot(cotangent_all, w_down, ((1,), (0,)))
    grad_gate = (grad_act * up * sigma * (1.0 + gate * (1.0 - sigma))).astype(BF16)
    grad_up = (grad_act * gate * sigma).astype(BF16)
    spread_two = dot(grad_gate, w_gate, ((1,), (1,))) + dot(grad_up, w_up, ((1,), (1,)))
    scaled_two = unshuffle(scatter_head(spread_two)).astype(F32)
    gate_sum = scatter_seq(dot(normed_two_all, grad_gate, ((0,), (0,))))
    up_sum = scatter_seq(dot(normed_two_all, grad_up, ((0,), (0,))))
    mixed = unshuffle(scatter_head(dot(act, w_down, ((1,), (1,)))))
    mixed_out = (hidden + mixed.astype(F32)).astype(BF16)

    grad_hidden = cotangent.astype(F32) + scale_two * (
        scaled_two - normed_two * jnp.mean(scaled_two * normed_two, axis=-1, keepdims=True)
    )
    grad_hidden_all = gather_head(grad_hidden.astype(BF16))
    grad_attended = dot(grad_hidden_all, w_o, ((1,), (1,))).astype(BF16)
    o_sum = scatter_seq(dot(attended, grad_hidden_all, ((0,), (0,))))
    grad_query, grad_keys, grad_values = attend_back(
        query, key_heads, value_heads, grad_attended, lse, place_q, place_k
    )
    grad_keys = from_slices(grad_keys, nh)
    grad_values = from_slices(grad_values, nh)
    scaled_one = unshuffle(scatter_head(dot(grad_query, w_q, ((1,), (1,))))).astype(F32)
    q_sum = scatter_seq(dot(normed_one_all, grad_query, ((0,), (0,))))
    grad_tokens = grad_hidden + scale_one * (
        scaled_one - normed_one * jnp.mean(scaled_one * normed_one, axis=-1, keepdims=True)
    )
    q_sum = from_slices(q_sum, nh).astype(F32)
    gate_sum = from_slices(gate_sum, nh).astype(F32)
    up_sum = from_slices(up_sum, nh).astype(F32)
    down_sum = from_slices(down_sum, nh).astype(F32)
    grad_gain_one = jnp.sum(q_weight.astype(F32) * q_sum, axis=1)
    grad_gain_two = jnp.sum(
        gate_weight.astype(F32) * gate_sum + up_weight.astype(F32) * up_sum, axis=1
    )
    return (
        mixed_out,
        grad_tokens.astype(BF16),
        grad_keys,
        grad_values,
        gain_one * q_sum,
        o_sum.astype(F32),
        gain_two * gate_sum,
        gain_two * up_sum,
        down_sum.T,
        grad_gain_one,
        grad_gain_two,
    )


def solution(mesh):
    both = ("head", "seq")
    rows, cols, line, own = P(both, None), P(None, both), P(both), P("seq", None)
    return jax.shard_map(
        functools.partial(per_device, mesh.shape["head"], mesh.shape["seq"]),
        mesh=mesh,
        in_specs=(rows,) * 7 + (cols, line, line, own, own, rows),
        out_specs=(rows,) * 8 + (cols, line, line),
        check_vma=False,
    )
```

time: 4500 us -> 926 us (0.21)
  waiting for transfers between devices: 4110 us -> 600 us
  matrix products: 241 us -> 86.3 us
    reduce_scatter x5 -> x9, waiting for transfers between devices: 3590 us -> 306 us  [the longest x4 157 us: scatter_head(): lax.psum_scatter(full.astype(BF16), 'head', scatter_dimension=0, tiled=True)]
    all_gather x5 -> x9, waiting for transfers between devices: 460 us -> 281 us  [the longest x5 151 us: gather_seq(): return lax.all_gather(part, 'seq', axis=0, tiled=True)]
    dot_general x29 -> x15, matrix products: 241 us -> 86.3 us  [dot(): lax.dot_general(left, right, (dims, ((), ())), preferred_element_type=F32)]
    all_to_all x1 -> x5, blocking collectives: 12.2 us -> 76 us  [the longest x4 59.6 us: to_slices(): lax.all_to_all(parts, 'head', 0, 0, tiled=False)]
    unnamed x1 -> x0, blocking collectives: 45.1 us -> none
  transfers between devices with their start and end apart: 18 -> 25, of which waited for: 15 -> 19; matrix products, arithmetic and copies ran while one was open for 3% -> 14% of each run, Pallas kernels for 0% -> 2%
where the time goes in v1:
time: 926 us; the launch traced here: 916 us
  waiting for transfers between devices  600 us (65%)
  matrix products  86.3 us (9%)
  blocking collectives  76 us (8%)
  local copies, waits for them, and re-layouts  62.8 us (7%)
  starting transfers between devices  27.5 us (3%)
  other arithmetic  26.8 us (3%)
  Pallas kernels  21 us (2%)
  between operations  15.3 us (2%)
    reduce_scatter x4, waiting for transfers between devices, scatter_head(): lax.psum_scatter(full.astype(BF16), 'head', scatter_dimension=0, tiled=True)  157 us
    all_gather x5, waiting for transfers between devices, gather_seq(): return lax.all_gather(part, 'seq', axis=0, tiled=True)  151 us
    reduce_scatter x5, waiting for transfers between devices, scatter_seq(): lax.psum_scatter(full.astype(BF16), 'seq', scatter_dimension=0, tiled=True)  148 us
    all_gather x4, waiting for transfers between devices, gather_head(): return lax.all_gather(part, 'head', axis=0, tiled=True)  131 us
    dot_general x15, matrix products, dot(): lax.dot_general(left, right, (dims, ((), ())), preferred_element_type=F32)  86.3 us
    all_to_all x4, blocking collectives, to_slices(): lax.all_to_all(parts, 'head', 0, 0, tiled=False)  59.6 us
    all_to_all x5, starting transfers between devices, from_slices(): parts = lax.all_to_all(parts, 'head', 0, 0, tiled=False)  19.1 us
  transfers between devices with their start and end apart: 25, of which 19 were waited for; matrix products, arithmetic and copies ran while one was open for 14% of the time, Pallas kernels for 2%

profile of v1, /device:TPU:0, one launch (start us, length us, event | category | flops | bytes accessed | tf_op | source)
XLA Modules:
  0.0 915.7 jit_solution(12249347663803250540)
XLA Ops:
  9.1 12.1 %all_to_all.60 = bf16[8,64,256]{2,1,0:T(8,128)(2,1)} all-to-all(bf16[8,64,256]{2,1,0:T(8,128)(2,1)S(1)} %copy.135), channel_id=1, replica_groups=mesh['head'=8,'seq'=4] {'head'}, dimensions={0} | all-to-all | bytes 524288 | tf_op jit(solution)/shard_map/all_to_all | solution.py:147
  24.8 3.5 all-to-all-start.1
  30.5 7.4 all-to-all-done.1
  38.0 3.5 all-to-all-start.2
  41.5 7.3 all-gather.12.cloned.1.call-done
  48.8 39.4 %all-gather.10.cloned.1.call-done = bf16[1024,2048]{0,1:T(8,128)(2,1)} async-done(((bf16[128,2048]{0,1:T(8,128)(2,1)}), bf16[1024,2048]{0,1:T(8,128)(2,1)}) %all-gather.10.cloned.1.call-update) | async-done | bytes 4194320 | tf_op jit(solution)/shard_map/all_gather | solution.py:166
  88.2 3.8 convolution_convert_fusion.9.q_ref
  92.0 7.5 attend.1
  100.5 17.2 %all-gather.14.cloned.1.call-done = bf16[256,2048]{1,0:T(8,128)(2,1)} async-done(((bf16[64,2048]{1,0:T(8,128)(2,1)}), bf16[256,2048]{1,0:T(8,128)(2,1)}) %all-gather.14.cloned.1.call-update) | async-done | bytes 1048592 | tf_op jit(solution)/shard_map/all_gather | solution.py:158
  117.7 4.5 convolution_convert_fusion.2
  130.1 16.1 %all_to_all.61 = bf16[8,64,688]{2,1,0:T(8,128)(2,1)} all-to-all(bf16[8,64,688]{2,1,0:T(8,128)(2,1)S(1)} %bitcast.134), channel_id=1, replica_groups=mesh['head'=8,'seq'=4] {'head'}, dimensions={0} | all-to-all | bytes 1409024 | tf_op jit(solution)/shard_map/all_to_all | solution.py:147
  146.3 26.9 %reduce-scatter.10.cloned.1.call-done = bf16[128,2048]{1,0:T(8,128)(2,1)} async-done(((bf16[1024,2048]{1,0:T(8,128)(2,1)}), bf16[128,2048]{1,0:T(8,128)(2,1)}) %reduce-scatter.10.cloned.1.call-update) | async-done | bytes 524304 | tf_op jit(solution)/shard_map/reduce_scatter | solution.py:170
  185.0 15.7 %all_to_all.62 = bf16[8,64,688]{2,1,0:T(8,128)(2,1)} all-to-all(bf16[8,64,688]{2,1,0:T(8,128)(2,1)S(1)} %bitcast.135), channel_id=1, replica_groups=mesh['head'=8,'seq'=4] {'head'}, dimensions={0} | all-to-all | bytes 1409024 | tf_op jit(solution)/shard_map/all_to_all | solution.py:147
  205.2 15.7 %all_to_all.63 = bf16[8,64,688]{2,1,0:T(8,128)(2,1)} all-to-all(bf16[8,64,688]{2,1,0:T(8,128)(2,1)S(1)} %bitcast.136), channel_id=1, replica_groups=mesh['head'=8,'seq'=4] {'head'}, dimensions={0} | all-to-all | bytes 1409024 | tf_op jit(solution)/shard_map/all_to_all | solution.py:147
  225.4 12.9 %all-gather.20.cloned.1.call-done = bf16[2048,688]{1,0:T(8,128)(2,1)} async-done(((bf16[512,688]{1,0:T(8,128)(2,1)}), bf16[2048,688]{1,0:T(8,128)(2,1)}) %all-gather.20.cloned.1.call-update) | async-done | bytes 2818064 | tf_op jit(solution)/shard_map/all_gather | solution.py:158
  238.2 38.6 %all-gather.16.cloned.1.call-done = bf16[1024,2048]{0,1:T(8,128)(2,1)} async-done(((bf16[128,2048]{0,1:T(8,128)(2,1)}), bf16[1024,2048]{0,1:T(8,128)(2,1)}) %all-gather.16.cloned.1.call-update) | async-done | bytes 4194320 | tf_op jit(solution)/shard_map/all_gather | solution.py:166
  276.8 7.9 fusion.30
  284.8 57.3 %all-gather.18.cloned.1.call-done = bf16[2048,688]{1,0:T(8,128)(2,1)} async-done(((bf16[512,688]{1,0:T(8,128)(2,1)}), bf16[2048,688]{1,0:T(8,128)(2,1)}) %all-gather.18.cloned.1.call-update) | async-done | bytes 2818064 | tf_op jit(solution)/shard_map/all_gather | solution.py:158
  342.0 7.9 fusion.29
  349.9 56.0 %all-gather.22.cloned.1.call-done = bf16[2048,688]{1,0:T(8,128)(2,1)} async-done(((bf16[512,688]{1,0:T(8,128)(2,1)}), bf16[2048,688]{1,0:T(8,128)(2,1)}) %all-gather.22.cloned.1.call-update) | async-done | bytes 2818064 | tf_op jit(solution)/shard_map/all_gather | solution.py:158
  405.8 38.7 %all-gather.24.cloned.1.call-done = bf16[1024,2048]{0,1:T(8,128)(2,1)} async-done(((bf16[128,2048]{0,1:T(8,128)(2,1)}), bf16[1024,2048]{0,1:T(8,128)(2,1)}) %all-gather.24.cloned.1.call-update) | async-done | bytes 4194320 | tf_op jit(solution)/shard_map/all_gather | solution.py:166
  444.6 10.3 %multiply_convert_fusion = (bf16[1024,688]{0,1:T(8,128)(2,1)S(1)}, bf16[1024,688]{0,1:T(8,128)(2,1)S(1)}, bf16[1024,688]{0,1:T(8,128)(2,1)}) fusion(f32[1024,688]{0,1:T(8,128)} %fusion.29, f32[1024,688]{0,1:T(8,128)} %fusion.30, bf16[1024,2048]{0,1:T(8,128)(2,1)} %all-gather.24.cloned.1.call-done, bf16[2048,688]{1,0:T(8,128)(2,1)} %all-gather.22.cloned.1.call-done), kind=kOutput, calls=%fused_computation.8 | convolution fusion | flops 2896953344 | bytes 16875520 | tf_op jit(solution)/shard_map/dot_general | solution.py:22
  454.9 3.7 fusion.31
  458.7 5.2 add_convert_fusion
  463.9 51.4 %reduce-scatter.14.cloned.1.call-done = bf16[128,2048]{1,0:T(8,128)(2,1)} async-done(((bf16[1024,2048]{1,0:T(8,128)(2,1)}), bf16[128,2048]{1,0:T(8,128)(2,1)}) %reduce-scatter.14.cloned.1.call-update) | async-done | bytes 524304 | tf_op jit(solution)/shard_map/reduce_scatter | solution.py:170
  526.7 7.3 fusion
  534.0 7.5 convolution_convert_fusion.4
  541.8 7.4 convolution_convert_fusion.5
  549.3 14.2 %all-gather.26.cloned.1.call-done = bf16[1024,2048]{1,0:T(8,128)(2,1)} async-done(((bf16[128,2048]{1,0:T(8,128)(2,1)}), bf16[1024,2048]{1,0:T(8,128)(2,1)}) %all-gather.26.cloned.1.call-update) | async-done | bytes 4194320 | tf_op jit(solution)/shard_map/all_gather | solution.py:166
  563.5 3.8 convolution_convert_fusion.8.do_ref
  568.5 13.4 %attend_back.1 = (bf16[1024,256]{1,0:T(8,128)(2,1)S(1)}, bf16[1024,256]{1,0:T(8,128)(2,1)}, bf16[1024,256]{1,0:T(8,128)(2,1)}) custom-call(bf16[1024,256]{1,0:T(8,128)(2,1)S(1)} %convolution_convert_fusion.9.q_ref, bf16[1024,256]{1,0:T(8,128)(2,1)S(1)} %bitcast.121, bf16[1024,256]{1,0:T(8,128)(2,1)S(1)} %bitcast.123, ...), custom_call_target="tpu_custom_call" | custom-call | flops 2684354560 | bytes 4718592 | tf_op jit(solution)/shard_map/attend_back/pallas_call | solution.py:119
  584.2 7.1 convolution_convert_fusion.1
  591.4 4.5 convolution_convert_fusion.6
  596.0 3.2 convolution_convert_fusion
  599.3 21.6 %reduce-scatter.26.cloned.1.call-done = bf16[512,688]{0,1:T(8,128)(2,1)} async-done(((bf16[2048,688]{0,1:T(8,128)(2,1)}), bf16[512,688]{0,1:T(8,128)(2,1)}) %reduce-scatter.26.cloned.1.call-update) | async-done | bytes 704528 | tf_op jit(solution)/shard_map/reduce_scatter | solution.py:162
  623.1 3.7 all-to-all-start.11
  626.8 51.5 %reduce-scatter.24.cloned.1.call-done = bf16[512,688]{0,1:T(8,128)(2,1)} async-done(((bf16[2048,688]{0,1:T(8,128)(2,1)}), bf16[512,688]{0,1:T(8,128)(2,1)}) %reduce-scatter.24.cloned.1.call-update) | async-done | bytes 704528 | tf_op jit(solution)/shard_map/reduce_scatter | solution.py:162
  680.5 3.7 all-to-all-start.10
  684.2 51.3 %reduce-scatter.22.cloned.1.call-done = bf16[512,688]{0,1:T(8,128)(2,1)} async-done(((bf16[2048,688]{0,1:T(8,128)(2,1)}), bf16[512,688]{0,1:T(8,128)(2,1)}) %reduce-scatter.22.cloned.1.call-update) | async-done | bytes 704528 | tf_op jit(solution)/shard_map/reduce_scatter | solution.py:162
  736.9 16.4 %all_to_all.64 = bf16[8,64,688]{2,1,0:T(8,128)(2,1)} all-to-all(bf16[8,64,688]{2,1,0:T(8,128)(2,1)S(1)} %bitcast.133), channel_id=1, replica_groups=mesh['head'=8,'seq'=4] {'head'}, dimensions={0} | all-to-all | bytes 1409024 | tf_op jit(solution)/shard_map/all_to_all | solution.py:153
  753.3 3.5 all-to-all-start.7
  761.9 4.6 all-to-all-done.7
  766.4 4.2 all-to-all-start.6
  780.4 4.2 all-to-all-start.8
  784.6 3.9 fusion.6
  788.5 30.0 %reduce-scatter.12.cloned.1.call-done = bf16[128,2048]{1,0:T(8,128)(2,1)} async-done(((bf16[1024,2048]{1,0:T(8,128)(2,1)}), bf16[128,2048]{1,0:T(8,128)(2,1)}) %reduce-scatter.12.cloned.1.call-update) | async-done | bytes 524304 | tf_op jit(solution)/shard_map/reduce_scatter | solution.py:170
  824.0 24.0 %reduce-scatter.20.cloned.1.call-done = bf16[64,2048]{1,0:T(8,128)(2,1)} async-done(((bf16[256,2048]{1,0:T(8,128)(2,1)}), bf16[64,2048]{1,0:T(8,128)(2,1)}) %reduce-scatter.20.cloned.1.call-update) | async-done | bytes 262160 | tf_op jit(solution)/shard_map/reduce_scatter | solution.py:162
  852.3 48.9 %reduce-scatter.16.cloned.1.call-done = bf16[128,2048]{1,0:T(8,128)(2,1)} async-done(((bf16[1024,2048]{1,0:T(8,128)(2,1)}), bf16[128,2048]{1,0:T(8,128)(2,1)}) %reduce-scatter.16.cloned.1.call-update) | async-done | bytes 524304 | tf_op jit(solution)/shard_map/reduce_scatter | solution.py:170
  (160 shorter events, 90.3 us)
Async XLA Ops:
  7.2 15.4 %copy-start.2 = (bf16[128,2048]{1,0:T(8,128)(2,1)S(1)}, bf16[128,2048]{1,0:T(8,128)(2,1)}, u32[]{:S(2)}) copy-start(bf16[128,2048]{1,0:T(8,128)(2,1)} %param.13) | copy-start | bytes 1572868
  7.2 41.6 %all-gather.12.cloned.1.call-start = ((), (), s32[]{:S(2)}) async-start(), calls=%async_computation.22 | async-start | bytes 1310720 | tf_op jit(solution)/shard_map/all_gather | solution.py:158
  9.1 14.9 %copy-start.13 = (bf16[128,2048]{1,0:T(8,128)(2,1)S(1)}, bf16[128,2048]{1,0:T(8,128)(2,1)}, u32[]{:S(2)}) copy-start(bf16[128,2048]{1,0:T(8,128)(2,1)} %param.14) | copy-start | bytes 1572868
  21.3 66.9 %all-gather.10.cloned.1.call-start = ((), (), s32[]{:S(2)}) async-start(), calls=%async_computation.21 | async-start | bytes 4718592 | tf_op jit(solution)/shard_map/all_gather | solution.py:166
  22.6 6.4 copy-start.19
  22.6 6.6 copy-start.15
  22.8 6.9 copy-start.14
  24.8 13.2 %all-to-all-start.1 = ((bf16[8,128,256]{2,1,0:T(8,128)(2,1)}), bf16[8,128,256]{2,1,0:T(8,128)(2,1)S(1)}, u32[]{:S(2)}, u32[]{:S(2)}) async-start(bf16[8,128,256]{2,1,0:T(8,128)(2,1)} %bitcast.119), calls=%async_computation.1 | async-start | bytes 1048576 | tf_op jit(solution)/shard_map/all_to_all | solution.py:147
  28.3 89.4 %all-gather.14.cloned.1.call-start = ((), (), s32[]{:S(2)}) async-start(), calls=%async_computation.23 | async-start | bytes 1310720 | tf_op jit(solution)/shard_map/all_gather | solution.py:158
  38.0 54.0 %all-to-all-start.2 = ((bf16[8,128,256]{2,1,0:T(8,128)(2,1)}), bf16[8,128,256]{2,1,0:T(8,128)(2,1)S(1)}, u32[]{:S(2)}, u32[]{:S(2)}) async-start(bf16[8,128,256]{2,1,0:T(8,128)(2,1)} %bitcast.117), calls=%async_computation.2 | async-start | bytes 1048576 | tf_op jit(solution)/shard_map/all_to_all | solution.py:147
  41.5 131.8 %reduce-scatter.10.cloned.1.call-start = ((), (), s32[]{:S(2)}) async-start(), calls=%async_computation.24 | async-start | bytes 4718592 | tf_op jit(solution)/shard_map/reduce_scatter | solution.py:170
  99.5 1.0 copy-start
  122.2 116.0 %all-gather.20.cloned.1.call-start = ((), (), s32[]{:S(2)}) async-start(), calls=%async_computation.27 | async-start | bytes 3932160 | tf_op jit(solution)/shard_map/all_gather | solution.py:158
  146.2 130.6 %all-gather.16.cloned.1.call-start = ((), (), s32[]{:S(2)}) async-start(), calls=%async_computation.25 | async-start | bytes 4718592 | tf_op jit(solution)/shard_map/all_gather | solution.py:166
  180.5 161.5 %all-gather.18.cloned.1.call-start = ((), (), s32[]{:S(2)}) async-start(), calls=%async_computation.26 | async-start | bytes 3932160 | tf_op jit(solution)/shard_map/all_gather | solution.py:158
  200.7 205.1 %all-gather.22.cloned.1.call-start = ((), (), s32[]{:S(2)}) async-start(), calls=%async_computation.28 | async-start | bytes 3932160 | tf_op jit(solution)/shard_map/all_gather | solution.py:158
  220.9 223.7 %all-gather.24.cloned.1.call-start = ((), (), s32[]{:S(2)}) async-start(), calls=%async_computation.30 | async-start | bytes 4718592 | tf_op jit(solution)/shard_map/all_gather | solution.py:166
  224.9 290.5 %reduce-scatter.14.cloned.1.call-start = ((), (), s32[]{:S(2)}) async-start(), calls=%async_computation.31 | async-start | bytes 4718592 | tf_op jit(solution)/shard_map/reduce_scatter | solution.py:170
  444.6 10.3 %copy-start.18 = (bf16[2048,688]{1,0:T(8,128)(2,1)S(1)}, bf16[2048,688]{1,0:T(8,128)(2,1)}, u32[]{:S(2)}) copy-start(bf16[2048,688]{1,0:T(8,128)(2,1)} %all-gather.18.cloned.1.call-done) | copy-start | bytes 8454148
  454.9 3.7 copy-start.21
  454.9 3.7 copy-start.23
  454.9 3.7 copy-start.17
  463.9 99.6 %all-gather.26.cloned.1.call-start = ((), (), s32[]{:S(2)}) async-start(), calls=%async_computation.32 | async-start | bytes 4718592 | tf_op jit(solution)/shard_map/all_gather | solution.py:166
  522.4 1.8 copy-start.4
  526.6 94.2 %reduce-scatter.26.cloned.1.call-start = ((), (), s32[]{:S(2)}) async-start(), calls=%async_computation.38 | async-start | bytes 3522560 | tf_op jit(solution)/shard_map/reduce_scatter | solution.py:162
  534.0 144.3 %reduce-scatter.24.cloned.1.call-start = ((), (), s32[]{:S(2)}) async-start(), calls=%async_computation.37 | async-start | bytes 3522560 | tf_op jit(solution)/shard_map/reduce_scatter | solution.py:162
  541.6 193.9 %reduce-scatter.22.cloned.1.call-start = ((), (), s32[]{:S(2)}) async-start(), calls=%async_computation.36 | async-start | bytes 3522560 | tf_op jit(solution)/shard_map/reduce_scatter | solution.py:162
  549.2 231.2 %reduce-scatter.18.cloned.1.call-start = ((), (), s32[]{:S(2)}) async-start(), calls=%async_computation.34 | async-start | bytes 1310720 | tf_op jit(solution)/shard_map/reduce_scatter | solution.py:162
  567.2 1.2 copy-start.1
  568.5 13.4 %copy-start.16 = (bf16[1024,2048]{0,1:T(8,128)(2,1)S(1)}, bf16[1024,2048]{0,1:T(8,128)(2,1)}, u32[]{:S(2)}) copy-start(bf16[1024,2048]{0,1:T(8,128)(2,1)} %all-gather.10.cloned.1.call-done) | copy-start | bytes 12582916
  581.9 2.3 copy-start.22
  584.2 234.4 %reduce-scatter.12.cloned.1.call-start = ((), (), s32[]{:S(2)}) async-start(), calls=%async_computation.29 | async-start | bytes 4718592 | tf_op jit(solution)/shard_map/reduce_scatter | solution.py:170
  591.3 4.7 copy-start.11
  591.3 256.6 %reduce-scatter.20.cloned.1.call-start = ((), (), s32[]{:S(2)}) async-start(), calls=%async_computation.35 | async-start | bytes 1310720 | tf_op jit(solution)/shard_map/reduce_scatter | solution.py:162
  595.9 305.2 %reduce-scatter.16.cloned.1.call-start = ((), (), s32[]{:S(2)}) async-start(), calls=%async_computation.33 | async-start | bytes 4718592 | tf_op jit(solution)/shard_map/reduce_scatter | solution.py:170
  623.1 57.4 %all-to-all-start.11 = ((bf16[8,64,688]{2,1,0:T(8,128)(2,1)}), bf16[8,64,688]{2,1,0:T(8,128)(2,1)S(1)}, u32[]{:S(2)}, u32[]{:S(2)}) async-start(bf16[8,64,688]{2,1,0:T(8,128)(2,1)} %bitcast.49), calls=%async_computation.20 | async-start | bytes 1572864 | tf_op jit(solution)/shard_map/all_to_all | solution.py:153
  680.5 56.3 %all-to-all-start.10 = ((bf16[8,64,688]{2,1,0:T(8,128)(2,1)}), bf16[8,64,688]{2,1,0:T(8,128)(2,1)S(1)}, u32[]{:S(2)}, u32[]{:S(2)}) async-start(bf16[8,64,688]{2,1,0:T(8,128)(2,1)} %bitcast.46), calls=%async_computation.18 | async-start | bytes 1572864 | tf_op jit(solution)/shard_map/all_to_all | solution.py:153
  736.9 16.4 %copy-start.7 = (bf16[8,64,688]{2,1,0:T(8,128)(2,1)}, bf16[8,64,688]{2,1,0:T(8,128)(2,1)S(1)}, u32[]{:S(2)}) copy-start(bf16[8,64,688]{2,1,0:T(8,128)(2,1)S(1)} %all-to-all-done.10) | copy-start | bytes 2113540
  753.3 13.2 %all-to-all-start.7 = ((bf16[8,128,256]{2,1,0:T(8,128)(2,1)}), bf16[8,128,256]{2,1,0:T(8,128)(2,1)S(1)}, u32[]{:S(2)}, u32[]{:S(2)}) async-start(bf16[8,128,256]{2,1,0:T(8,128)(2,1)} %bitcast.40), calls=%async_computation.11 | async-start | bytes 1048576 | tf_op jit(solution)/shard_map/all_to_all | solution.py:153
  756.9 13.7 %copy-start.8 = (bf16[8,64,688]{2,1,0:T(8,128)(2,1)S(1)}, bf16[8,64,688]{2,1,0:T(8,128)(2,1)}, u32[]{:S(2)}) copy-start(bf16[8,64,688]{2,1,0:T(8,128)(2,1)} %all_to_all.64) | copy-start | bytes 2113540
  766.4 6.4 copy-start.9
  766.4 13.9 %all-to-all-start.6 = ((bf16[8,128,256]{2,1,0:T(8,128)(2,1)}), bf16[8,128,256]{2,1,0:T(8,128)(2,1)}, u32[]{:S(2)}, u32[]{:S(2)}) async-start(bf16[8,128,256]{2,1,0:T(8,128)(2,1)} %bitcast.38), calls=%async_computation.10 | async-start | bytes 1048576 | tf_op jit(solution)/shard_map/all_to_all | solution.py:153
  780.4 69.3 %all-to-all-start.8 = ((bf16[8,64,256]{2,1,0:T(8,128)(2,1)}), bf16[8,64,256]{2,1,0:T(8,128)(2,1)}, u32[]{:S(2)}, u32[]{:S(2)}) async-start(bf16[8,64,256]{2,1,0:T(8,128)(2,1)} %bitcast.154), calls=%async_computation.13 | async-start | bytes 524288 | tf_op jit(solution)/shard_map/all_to_all | solution.py:153
  788.5 32.8 %copy-start.10 = (bf16[8,128,256]{2,1,0:T(8,128)(2,1)S(1)}, bf16[8,128,256]{2,1,0:T(8,128)(2,1)}, u32[]{:S(2)}) copy-start(bf16[8,128,256]{2,1,0:T(8,128)(2,1)} %copy-done.9) | copy-start | bytes 1572868
  821.2 29.5 %copy-start.12 = (bf16[64,2048]{1,0:T(8,128)(2,1)S(1)}, bf16[64,2048]{1,0:T(8,128)(2,1)}, u32[]{:S(2)}) copy-start(bf16[64,2048]{1,0:T(8,128)(2,1)} %param.16) | copy-start | bytes 786436
  852.3 52.8 %copy-start.3 = (bf16[128,2048]{1,0:T(8,128)(2,1)S(1)}, bf16[128,2048]{1,0:T(8,128)(2,1)}, u32[]{:S(2)}) copy-start(bf16[128,2048]{1,0:T(8,128)(2,1)} %param.13) | copy-start | bytes 1572868
  902.4 3.0 copy-start.5
  902.4 3.0 copy-start.6
  (1 other events, 0.7 us)
Sparse Core Ops, SparseCore 0:
  21.4 27.2 all-gather.11
  51.2 36.9 all-gather.9
  89.7 27.9 all-gather.13
  122.4 50.8 reduce-scatter.9
  174.7 63.4 all-gather.19
  240.7 36.0 all-gather.15
  278.5 63.4 all-gather.17
  343.7 62.1 all-gather.21
  408.5 36.0 all-gather.23
  464.0 51.3 reduce-scatter.13
  526.7 36.6 all-gather.25
  565.6 55.1 reduce-scatter.25
  623.3 54.9 reduce-scatter.23
  680.5 54.9 reduce-scatter.21
  738.3 26.9 reduce-scatter.17
  768.5 49.9 reduce-scatter.11
  820.8 27.1 reduce-scatter.19
  851.1 49.9 reduce-scatter.15

commit v2 on v1

--- a/solution.py
+++ b/solution.py
@@ -9,6 +9,7 @@
 from jax.sharding import PartitionSpec as P
 
 HEAD_DIM = 128
+NH, NS = 8, 4
 EPS = 1e-06
 BF16 = jnp.bfloat16
 F32 = jnp.float32
@@ -141,17 +142,191 @@
     )(query, keys, values, grad, lse, place_q, place_k)
 
 
-def to_slices(weight, nh):
+MESH = pl.DeviceIdType.MESH
+ANY = pl.BlockSpec(memory_space=pl.ANY)
+VMEM = pl.BlockSpec(memory_space=pltpu.VMEM)
+
+
+def peers_of(nh):
+    h = lax.axis_index("head")
+    s = lax.axis_index("seq")
+    if nh == 8:
+        others = [lax.bitwise_xor(h, k) for k in range(1, 8)]
+    else:
+        others = [lax.rem(h + k, nh) for k in range(1, nh)]
+    return h, s, others
+
+
+def greet(s, others):
+    barrier = pltpu.get_barrier_semaphore()
+    for p in others:
+        pl.semaphore_signal(barrier, inc=1, device_id=(p, s), device_id_type=MESH)
+    pl.semaphore_wait(barrier, len(others))
+
+
+def ag_kernel(nh, x_ref, o_ref, send, recv, own):
+    h, s, others = peers_of(nh)
+    r = x_ref.shape[0]
+    half = r // 2
+
+    def put(i, src, dst, to):
+        cp = pltpu.make_async_remote_copy(src_ref=src, dst_ref=dst, send_sem=send.at[i], recv_sem=recv.at[i], device_id=(to, s), device_id_type=MESH)
+        cp.start()
+        return cp
+
+    mine = pltpu.make_async_copy(x_ref, o_ref.at[h], own)
+    mine.start()
+    greet(s, others)
+    if nh != 8:
+        cps = [put(i, x_ref, o_ref.at[h], p) for i, p in enumerate(others)]
+        for cp in cps:
+            cp.wait()
+        mine.wait()
+        return
+    pc, px, _, py, _, _, _ = others
+    pd = lax.bitwise_xor(h, 6)
+    lo, hi = pl.ds(0, half), pl.ds(half, half)
+    xa = put(0, x_ref.at[lo], o_ref.at[h, lo], px)
+    yb = put(1, x_ref.at[hi], o_ref.at[h, hi], py)
+    c0 = put(2, x_ref, o_ref.at[h], pc)
+    xb = put(3, x_ref.at[hi], o_ref.at[h, hi], px)
+    ya = put(4, x_ref.at[lo], o_ref.at[h, lo], py)
+    xa.wait_recv()
+    fy = put(5, o_ref.at[px, lo], o_ref.at[px, lo], py)
+    c1 = put(6, o_ref.at[px, lo], o_ref.at[px, lo], pc)
+    yb.wait_recv()
+    fx = put(7, o_ref.at[py, hi], o_ref.at[py, hi], px)
+    c2 = put(8, o_ref.at[py, hi], o_ref.at[py, hi], pc)
+    xb.wait_recv()
+    c3 = put(9, o_ref.at[px, hi], o_ref.at[px, hi], pc)
+    ya.wait_recv()
+    c4 = put(10, o_ref.at[py, lo], o_ref.at[py, lo], pc)
+    fy.wait_recv()
+    c5 = put(11, o_ref.at[pd, lo], o_ref.at[pd, lo], pc)
+    fx.wait_recv()
+    c6 = put(12, o_ref.at[pd, hi], o_ref.at[pd, hi], pc)
+    for cp in (c0, c1, c2, c3, c4, c5, c6):
+        cp.wait_recv()
+    for cp in (xa, yb, xb, ya, fy, fx, c0, c1, c2, c3, c4, c5, c6):
+        cp.wait_send()
+    mine.wait()
+
+
+def ag_head(x, nh, cid, name):
+    r, d = x.shape
+    return pl.pallas_call(
+        functools.partial(ag_kernel, nh),
+        out_shape=jax.ShapeDtypeStruct((nh, r, d), x.dtype),
+        in_specs=[ANY], out_specs=ANY,
+        scratch_shapes=[pltpu.SemaphoreType.DMA((16,)), pltpu.SemaphoreType.DMA((16,)), pltpu.SemaphoreType.DMA],
+        compiler_params=pltpu.CompilerParams(collective_id=cid, has_side_effects=True),
+        name=name,
+    )(x).reshape(nh * r, d)
+
+
+def rs_kernel(nh, p_ref, o_ref, core_in, held, far_in, send, recv):
+    h, s, others = peers_of(nh)
+
+    def put(i, src, dst, to):
+        cp = pltpu.make_async_remote_copy(src_ref=src, dst_ref=dst, send_sem=send.at[i], recv_sem=recv.at[i], device_id=(to, s), device_id_type=MESH)
+        cp.start()
+        return cp
+
+    greet(s, others)
+    if nh != 8:
+        cps = [put(i, p_ref.at[p], far_in.at[i], p) for i, p in enumerate(others)]
+        total = p_ref[h].astype(F32)
+        for i, cp in enumerate(cps):
+            cp.wait_recv()
+            total = total + far_in[i].astype(F32)
+        o_ref[...] = total
+        for cp in cps:
+            cp.wait_send()
+        return
+    pc = others[0]
+    ks = (6, 2, 4, 0)
+    near = [put(i, p_ref.at[lax.bitwise_xor(pc, k)], core_in.at[i], pc) for i, k in enumerate(ks)]
+    far = []
+    for i, k in enumerate(ks):
+        near[i].wait_recv()
+        to = lax.bitwise_xor(h, k)
+        total = p_ref[to].astype(F32) + core_in[i].astype(F32)
+        if k:
+            held[i] = total.astype(BF16)
+            far.append(put(4 + i, held.at[i], far_in.at[i], to))
+        else:
+            o_ref[...] = total
+    for i in (1, 2, 0):
+        far[i].wait_recv()
+        o_ref[...] += far_in[i].astype(F32)
+    for cp in near + far:
+        cp.wait_send()
+
+
+def rs_head(x, nh, cid, name):
+    n, d = x.shape
+    r = n // nh
+    near = 4 if nh == 8 else 1
+    return pl.pallas_call(
+        functools.partial(rs_kernel, nh),
+        out_shape=jax.ShapeDtypeStruct((r, d), F32),
+        in_specs=[VMEM], out_specs=VMEM,
+        scratch_shapes=[pltpu.VMEM((near, r, d), BF16), pltpu.VMEM((3, r, d), BF16), pltpu.VMEM((3 if nh == 8 else nh - 1, r, d), BF16),
+                        pltpu.SemaphoreType.DMA((16,)), pltpu.SemaphoreType.DMA((16,))],
+        compiler_params=pltpu.CompilerParams(collective_id=cid, has_side_effects=True, vmem_limit_bytes=48 << 20),
+        name=name,
+    )(x.reshape(nh, r, d))
+
+
+def a2a_kernel(nh, m, *refs):
+    xs, os, (send, recv, own) = refs[:m], refs[m:2 * m], refs[2 * m:]
+    h, s, others = peers_of(nh)
+    mine = [pltpu.make_async_copy(x.at[h], o.at[h], own.at[j]) for j, (x, o) in enumerate(zip(xs, os))]
+    for cp in mine:
+        cp.start()
+    greet(s, others)
+    cps = []
+    order = [5, 1, 3, 0, 4, 2, 6] if nh == 8 else range(nh - 1)
+    for j, (x, o) in enumerate(zip(xs, os)):
+        for i in order:
+            p = others[i]
+            cp = pltpu.make_async_remote_copy(src_ref=x.at[p], dst_ref=o.at[h], send_sem=send.at[j, i], recv_sem=recv.at[j, i], device_id=(p, s), device_id_type=MESH)
+            cp.start()
+            cps.append(cp)
+    for cp in cps:
+        cp.wait()
+    for cp in mine:
+        cp.wait()
+
+
+def a2a_head(xs, nh, cid, name):
+    m = len(xs)
+    return pl.pallas_call(
+        functools.partial(a2a_kernel, nh, m),
+        out_shape=[jax.ShapeDtypeStruct(x.shape, x.dtype) for x in xs],
+        in_specs=[ANY] * m, out_specs=[ANY] * m,
+        scratch_shapes=[pltpu.SemaphoreType.DMA((m, nh - 1)), pltpu.SemaphoreType.DMA((m, nh - 1)), pltpu.SemaphoreType.DMA((m,))],
+        compiler_params=pltpu.CompilerParams(collective_id=cid, has_side_effects=True),
+        name=name,
+    )(*xs)
+
+
+def slices_of(weight, nh):
     rows, cols = weight.shape
-    parts = weight.reshape(rows, nh, cols // nh).swapaxes(0, 1)
-    return lax.all_to_all(parts, "head", 0, 0, tiled=False).reshape(nh * rows, cols // nh)
-
-
-def from_slices(part, nh):
-    rows, cols = part.shape
-    parts = part.reshape(nh, rows // nh, cols)
-    parts = lax.all_to_all(parts, "head", 0, 0, tiled=False)
-    return parts.swapaxes(0, 1).reshape(rows // nh, nh * cols)
+    return weight.reshape(rows, nh, cols // nh).swapaxes(0, 1)
+
+
+def rows_of(parts):
+    nh, rows, cols = parts.shape
+    return parts.swapaxes(0, 1).reshape(rows, nh * cols)
+
+
+def flat(parts):
+    return parts.reshape(parts.shape[0] * parts.shape[1], parts.shape[2])
+
+
+def cut(part, nh):
+    return part.reshape(nh, part.shape[0] // nh, part.shape[1])
 
 
 def gather_seq(part):
@@ -162,12 +337,395 @@
     return lax.psum_scatter(full.astype(BF16), "seq", scatter_dimension=0, tiled=True)
 
 
-def gather_head(part):
-    return lax.all_gather(part, "head", axis=0, tiled=True)
-
-
-def scatter_head(full):
-    return lax.psum_scatter(full.astype(BF16), "head", scatter_dimension=0, tiled=True)
+def remote(src, dst, send, recv, to):
+    return pltpu.make_async_remote_copy(
+        src_ref=src, dst_ref=dst, send_sem=send, recv_sem=recv, device_id=to, device_id_type=MESH
+    )
+
+
+class Net:
+    def __init__(self):
+        self.h = lax.axis_index("head")
+        self.s = lax.axis_index("seq")
+        self.open = []
+
+    def peer(self, k):
+        return (lax.bitwise_xor(self.h, k), self.s)
+
+    def greet(self):
+        barrier = pltpu.get_barrier_semaphore()
+        for k in range(1, NH):
+            pl.semaphore_signal(barrier, inc=1, device_id=self.peer(k), device_id_type=MESH)
+        for k in range(1, NS):
+            there = (self.h, lax.rem(self.s + k, NS))
+            pl.semaphore_signal(barrier, inc=1, device_id=there, device_id_type=MESH)
+        pl.semaphore_wait(barrier, NH - 1 + NS - 1)
+
+    def put(self, src, dst, send, recv, to):
+        copy = remote(src, dst, send, recv, to)
+        copy.start()
+        self.open.append(copy)
+        return copy
+
+    def swap(self, src, dst, send, recv, own):
+        mine = pltpu.make_async_copy(src.at[self.h], dst(self.h), own)
+        mine.start()
+        copies = []
+        for k in (6, 2, 4, 1, 5, 3, 7):
+            to = self.peer(k)
+            copies.append(
+                self.put(src.at[to[0]], dst(self.h), send.at[k - 1], recv.at[k - 1], to)
+            )
+
+        def finish():
+            for copy in copies:
+                copy.wait_recv()
+            mine.wait()
+
+        return finish
+
+    def gather(self, src, dst, send, recv, own):
+        half = src.shape[0] // 2
+        lo, hi = pl.ds(0, half), pl.ds(half, half)
+        h, core, px, py = self.h, self.peer(1), self.peer(2), self.peer(4)
+        x, y, d = px[0], py[0], lax.bitwise_xor(h, 6)
+        mine = pltpu.make_async_copy(src, dst.at[h], own)
+        mine.start()
+
+        def put(i, a, b, to):
+            return self.put(a, b, send.at[i], recv.at[i], to)
+
+        xa = put(0, src.at[lo], dst.at[h, lo], px)
+        yb = put(1, src.at[hi], dst.at[h, hi], py)
+        c0 = put(2, src, dst.at[h], core)
+        xb = put(3, src.at[hi], dst.at[h, hi], px)
+        ya = put(4, src.at[lo], dst.at[h, lo], py)
+
+        def finish():
+            near = [c0]
+            xa.wait_recv()
+            fy = put(5, dst.at[x, lo], dst.at[x, lo], py)
+            near.append(put(6, dst.at[x, lo], dst.at[x, lo], core))
+            yb.wait_recv()
+            fx = put(7, dst.at[y, hi], dst.at[y, hi], px)
+            near.append(put(8, dst.at[y, hi], dst.at[y, hi], core))
+            xb.wait_recv()
+            near.append(put(9, dst.at[x, hi], dst.at[x, hi], core))
+            ya.wait_recv()
+            near.append(put(10, dst.at[y, lo], dst.at[y, lo], core))
+            fy.wait_recv()
+            near.append(put(11, dst.at[d, lo], dst.at[d, lo], core))
+            fx.wait_recv()
+            near.append(put(12, dst.at[d, hi], dst.at[d, hi], core))
+            for copy in near:
+                copy.wait_recv()
+            mine.wait()
+
+        return finish
+
+    def scatter(self, block, near_out, core_in, held, far_in, send, recv):
+        core = self.peer(1)
+        order = (6, 2, 4, 0)
+        near, far = [], []
+        for i, k in enumerate(order):
+            near_out[i] = block(lax.bitwise_xor(core[0], k)).astype(BF16)
+            near.append(self.put(near_out.at[i], core_in.at[i], send.at[i], recv.at[i], core))
+        for i, k in enumerate(order):
+            total = block(lax.bitwise_xor(self.h, k))
+            near[i].wait_recv()
+            total = total + core_in[i].astype(F32)
+            if k:
+                held[i] = total.astype(BF16)
+                far.append(
+                    self.put(held.at[i], far_in.at[i], send.at[4 + i], recv.at[4 + i], self.peer(k))
+                )
+
+        def finish():
+            result = total
+            for i in (1, 2, 0):
+                far[i].wait_recv()
+                result = result + far_in[i].astype(F32)
+            return result
+
+        return finish
+
+    def z_gather(self, src, block, send, recv):
+        s = self.s
+        steps = (2, -2, 1, -1)
+
+        def there(d):
+            return (self.h, s + d)
+
+        def copy(n):
+            return remote(src, block(s), send.at[n], recv.at[s], there(steps[n]))
+
+        def valid(d):
+            return (s + d >= 0) & (s + d < NS)
+
+        middle = (s == 1) | (s == 2)
+        origin = jnp.where(s == 2, 0, NS - 1)
+        target = (self.h, NS - 1 - origin)
+
+        def relay():
+            return remote(block(origin), block(origin), send.at[4], recv.at[origin], target)
+
+        for n, d in enumerate(steps):
+
+            @pl.when(valid(d))
+            def _():
+                copy(n).start()
+
+        def forward():
+            @pl.when(middle)
+            def _():
+                relay().wait_recv()
+                relay().start()
+
+        def finish():
+            for t in range(NS):
+                waited = ((s == 2) & (t == 0)) | ((s == 1) & (t == NS - 1))
+
+                @pl.when((s != t) & jnp.logical_not(waited))
+                def _():
+                    remote(block(t), block(t), send.at[0], recv.at[t], (self.h, s)).wait_recv()
+
+        def drain():
+            for n, d in enumerate(steps):
+
+                @pl.when(valid(d))
+                def _():
+                    copy(n).wait_send()
+
+            @pl.when(middle)
+            def _():
+                relay().wait_send()
+
+        return forward, finish, drain
+
+    def close(self):
+        for copy in self.open:
+            copy.wait_send()
+
+
+def fetch(pairs, sems):
+    copies = [pltpu.make_async_copy(a, b, sems.at[i]) for i, (a, b) in enumerate(pairs)]
+    for copy in copies:
+        copy.start()
+    for copy in copies:
+        copy.wait()
+
+
+def forward_kernel(
+    q_own,
+    gate_own,
+    up_own,
+    down_own,
+    o_own,
+    n1_own,
+    k_own,
+    v_own,
+    cot_own,
+    tokens,
+    place_q,
+    place_k,
+    w_q,
+    w_gate,
+    w_up,
+    w_down,
+    w_o,
+    n1_all,
+    k_all,
+    v_all,
+    cot_all,
+    n2_all,
+    query,
+    attended,
+    lse,
+    hidden_out,
+    wq_v,
+    wo_v,
+    n1_v,
+    k_v,
+    v_v,
+    n2_v,
+    near_out,
+    core_in,
+    held,
+    far_in,
+    swap_send,
+    swap_recv,
+    ag_send,
+    ag_recv,
+    rs_send,
+    rs_recv,
+    z_send,
+    z_recv,
+    own,
+    fetch_sem,
+):
+    net = Net()
+    h, s = net.h, net.s
+    net.greet()
+
+    def swap(j, src, dst):
+        return net.swap(src, dst, swap_send.at[j], swap_recv.at[j], own.at[j])
+
+    def gather(j, src, dst):
+        return net.gather(src, dst, ag_send.at[j], ag_recv.at[j], own.at[8 + j])
+
+    def z_gather(j, src, block):
+        return net.z_gather(src, block, z_send.at[j], z_recv.at[j])
+
+    def slab(w):
+        return lambda t: w.at[:, t]
+
+    q_there = swap(0, q_own, lambda p: w_q.at[p, s])
+    n1_there = gather(0, n1_own, n1_all)
+    mine = pltpu.make_async_copy(o_own, w_o.at[s], own.at[15])
+    mine.start()
+    gate_there = swap(1, gate_own, lambda p: w_gate.at[p, s])
+    q_there()
+    zq = z_gather(0, w_q.at[:, s], slab(w_q))
+    k_there = swap(2, k_own, lambda p: k_all.at[p])
+    v_there = swap(3, v_own, lambda p: v_all.at[p])
+    n1_there()
+    gate_there()
+    zo = z_gather(1, o_own, lambda t: w_o.at[t])
+    zg = z_gather(2, w_gate.at[:, s], slab(w_gate))
+    up_there = swap(4, up_own, lambda p: w_up.at[p, s])
+    down_there = swap(5, down_own, lambda p: w_down.at[p, s])
+    zq[0]()
+    k_there()
+    v_there()
+    fetch([(n1_all, n1_v), (k_all, k_v), (v_all, v_v)], fetch_sem)
+    zq[1]()
+    fetch([(w_q, wq_v)], fetch_sem)
+
+    group = NH * n1_own.shape[0]
+    local = n1_own.shape[0]
+    width = n1_own.shape[1]
+    wide = query.shape[1]
+    step = 256
+    weight = wq_v[...].reshape(width, wide)
+
+    @pl.loop(0, group // step)
+    def _(i):
+        part = n1_v[pl.ds(i * (step // local), step // local)].reshape(step, width)
+        query[pl.ds(pl.multiple_of(i * step, step), step), :] = dot(
+            part, weight, ((1,), (0,))
+        ).astype(BF16)
+
+    up_there()
+    zu = z_gather(3, w_up.at[:, s], slab(w_up))
+    zo[0]()
+
+    scale = 1.0 / math.sqrt(HEAD_DIM)
+    for head in range(wide // HEAD_DIM):
+        cols = slice(head * HEAD_DIM, (head + 1) * HEAD_DIM)
+
+        @pl.loop(0, group // step)
+        def _(i):
+            rows = pl.ds(pl.multiple_of(i * step, step), step)
+            keys = k_v[:, :, cols].reshape(group, HEAD_DIM)
+            values = v_v[:, :, cols].reshape(group, HEAD_DIM)
+            raw = dot(query[rows, cols], keys, ((1,), (1,)))
+            allowed = (place_q[rows, 1:2] == place_k[1:2, :]) & (
+                place_k[0:1, :] <= place_q[rows, 0:1]
+            )
+            logits = jnp.where(allowed, raw * scale, -1e30)
+            top = jnp.max(logits, axis=-1, keepdims=True)
+            expo = jnp.exp(logits - top)
+            total = jnp.sum(expo, axis=-1, keepdims=True)
+            probs = (expo * (1.0 / total)).astype(BF16)
+            attended[rows, cols] = dot(probs, values, ((1,), (0,))).astype(BF16)
+            lse[rows, cols] = jnp.broadcast_to(top + jnp.log(total), (step, HEAD_DIM))
+
+    down_there()
+    zd = z_gather(4, w_down.at[:, s], slab(w_down))
+    zo[1]()
+    mine.wait()
+    fetch([(w_o, wo_v)], fetch_sem)
+
+    def o_block(p):
+        rows = pl.ds(pl.multiple_of(p * local, local), local)
+        return dot(attended[rows, :], wo_v[...].reshape(wide, width), ((1,), (0,)))
+
+    o_sum = net.scatter(o_block, near_out, core_in, held, far_in, rs_send, rs_recv)
+    zg[0]()
+    hidden = tokens[...].astype(F32) + o_sum()
+    hidden_out[...] = hidden
+    n2_v[...] = (hidden * rms_scale(hidden)).astype(BF16)
+    n2_there = gather(1, n2_v, n2_all)
+    n2_there()
+    cot_there = gather(2, cot_own, cot_all)
+    zu[0]()
+    cot_there()
+    zd[0]()
+    for z in (zg, zu, zd):
+        z[1]()
+    for z in (zq, zo, zg, zu, zd):
+        z[2]()
+    net.close()
+
+
+def forward_call(q_own, gate_own, up_own, down_own, o_own, n1_own, k_own, v_own, cot_own, tokens, place_q, place_k):
+    local, width = tokens.shape
+    group = NH * local
+    rows = o_own.shape[0]
+    wide, hid = q_own.shape[2], gate_own.shape[2]
+
+    def bf(*shape):
+        return jax.ShapeDtypeStruct(shape, BF16)
+
+    out_shape = [
+        bf(NH, NS, rows, wide),
+        bf(NH, NS, rows, hid),
+        bf(NH, NS, rows, hid),
+        bf(NH, NS, rows, hid),
+        bf(NS, rows, width),
+        bf(NH, local, width),
+        bf(NH, local, wide),
+        bf(NH, local, wide),
+        bf(NH, local, width),
+        bf(NH, local, width),
+        bf(group, wide),
+        bf(group, wide),
+        jax.ShapeDtypeStruct((group, wide), F32),
+        jax.ShapeDtypeStruct((local, width), F32),
+    ]
+    dma = pltpu.SemaphoreType.DMA
+    return pl.pallas_call(
+        forward_kernel,
+        out_shape=out_shape,
+        in_specs=[ANY] * 9 + [VMEM] * 3,
+        out_specs=[ANY] * 10 + [VMEM] * 4,
+        scratch_shapes=[
+            pltpu.VMEM((NH, NS, rows, wide), BF16),
+            pltpu.VMEM((NS, rows, width), BF16),
+            pltpu.VMEM((NH, local, width), BF16),
+            pltpu.VMEM((NH, local, wide), BF16),
+            pltpu.VMEM((NH, local, wide), BF16),
+            pltpu.VMEM((local, width), BF16),
+            pltpu.VMEM((4, local, width), BF16),
+            pltpu.VMEM((4, local, width), BF16),
+            pltpu.VMEM((3, local, width), BF16),
+            pltpu.VMEM((3, local, width), BF16),
+            dma((6, 7)),
+            dma((6, 7)),
+            dma((3, 13)),
+            dma((3, 13)),
+            dma((7,)),
+            dma((7,)),
+            dma((5, 5)),
+            dma((5, NS)),
+            dma((16,)),
+            dma((4,)),
+        ],
+        compiler_params=pltpu.CompilerParams(
+            collective_id=0, has_side_effects=True, vmem_limit_bytes=56 << 20
+        ),
+        name="forward",
+    )(q_own, gate_own, up_own, down_own, o_own, n1_own, k_own, v_own, cot_own, tokens, place_q, place_k)
 
 
 def per_device(
@@ -190,6 +748,144 @@
     local, width = tokens.shape
     rows = q_weight.shape[0]
 
+    def regroup(term):
+        cols = term.shape[1]
+        return term.reshape(nh, ns, rows, cols).swapaxes(0, 1).reshape(width, cols)
+
+    gain_one = attn_gain.astype(F32)[:, None]
+    gain_two = ffn_gain.astype(F32)[:, None]
+    inputs = tokens.astype(F32)
+    scale_one = rms_scale(inputs)
+    normed_one = inputs * scale_one
+    group = nh * local
+    position, segment = places(span_order[0], doc_lengths[0], group)
+    place_q = jnp.stack([position, segment], axis=1)
+    place_k = jnp.stack([position, segment], axis=0)
+    (w_q, w_gate, w_up, w_down, w_o, normed_one_all, key_heads, value_heads,
+     cotangent_all, normed_two_all, query, attended, lse, hidden) = forward_call(
+        slices_of((q_weight * gain_one).astype(BF16), nh),
+        slices_of((gate_weight * gain_two).astype(BF16), nh),
+        slices_of((up_weight * gain_two).astype(BF16), nh),
+        slices_of(down_weight.T, nh),
+        o_weight,
+        normed_one.astype(BF16),
+        slices_of(keys, nh),
+        slices_of(values, nh),
+        cotangent,
+        tokens,
+        place_q,
+        place_k,
+    )
+    w_q, w_gate, w_up, w_down = (w.reshape(width, w.shape[-1]) for w in (w_q, w_gate, w_up, w_down))
+    w_o = flat(w_o)
+    normed_one_all, key_heads, value_heads, cotangent_all, normed_two_all = (
+        flat(v) for v in (normed_one_all, key_heads, value_heads, cotangent_all, normed_two_all)
+    )
+    scale_two = rms_scale(hidden)
+    normed_two = hidden * scale_two
+    gate = dot(normed_two_all, w_gate, ((1,), (0,)))
+    up = dot(normed_two_all, w_up, ((1,), (0,)))
+    sigma = jax.nn.sigmoid(gate)
+    act = (gate * sigma * up).astype(BF16)
+    down_term = dot(cotangent_all, act, ((0,), (0,))).astype(BF16)
+    w_down, down_term = lax.optimization_barrier((w_down, down_term))
+    down_sum = scatter_seq(regroup(down_term))
+    grad_act = dot(cotangent_all, w_down, ((1,), (0,)))
+    grad_gate = (grad_act * up * sigma * (1.0 + gate * (1.0 - sigma))).astype(BF16)
+    grad_up = (grad_act * gate * sigma).astype(BF16)
+    spread_two = dot(grad_gate, w_gate, ((1,), (1,))) + dot(grad_up, w_up, ((1,), (1,)))
+    scaled_two = (rs_head(spread_two.astype(BF16), nh, 7, "sum_ffn"))
+    gate_term = dot(normed_two_all, grad_gate, ((0,), (0,))).astype(BF16)
+    up_term = dot(normed_two_all, grad_up, ((0,), (0,))).astype(BF16)
+    scaled_two, gate_term, up_term = lax.optimization_barrier((scaled_two, gate_term, up_term))
+    gate_sum = scatter_seq(regroup(gate_term))
+    up_sum = scatter_seq(regroup(up_term))
+
+    grad_hidden = cotangent.astype(F32) + scale_two * (
+        scaled_two - normed_two * jnp.mean(scaled_two * normed_two, axis=-1, keepdims=True)
+    )
+    grad_hidden_all = ag_head(grad_hidden.astype(BF16), nh, 8, "gather_dh")
+    grad_attended = dot(grad_hidden_all, w_o, ((1,), (1,))).astype(BF16)
+    o_sum = scatter_seq(dot(attended, grad_hidden_all, ((0,), (0,))))
+    grad_query, grad_keys, grad_values = attend_back(
+        query, key_heads, value_heads, grad_attended, lse, place_q, place_k
+    )
+    q_term = dot(normed_one_all, grad_query, ((0,), (0,))).astype(BF16)
+    grad_query, q_term = lax.optimization_barrier((grad_query, q_term))
+    q_sum = scatter_seq(regroup(q_term))
+    scaled_one = (rs_head(dot(grad_query, w_q, ((1,), (1,))).astype(BF16), nh, 9, "sum_q"))
+    grad_tokens = grad_hidden + scale_one * (
+        scaled_one - normed_one * jnp.mean(scaled_one * normed_one, axis=-1, keepdims=True)
+    )
+    mixed = (rs_head(dot(act, w_down, ((1,), (1,))).astype(BF16), nh, 10, "sum_mixed"))
+    mixed_out = (hidden + mixed).astype(BF16)
+    grad_keys, grad_values = a2a_head([cut(grad_keys, nh), cut(grad_values, nh)], nh, 11, "back_kv")
+    gate_sum, down_sum = a2a_head([cut(gate_sum, nh), cut(down_sum, nh)], nh, 12, "back_ffn")
+    q_sum, up_sum = a2a_head([cut(q_sum, nh), cut(up_sum, nh)], nh, 13, "back_q")
+    q_sum = rows_of(q_sum).astype(F32)
+    gate_sum = rows_of(gate_sum).astype(F32)
+    up_sum = rows_of(up_sum).astype(F32)
+    down_sum = rows_of(down_sum).astype(F32)
+    grad_gain_one = jnp.sum(q_weight.astype(F32) * q_sum, axis=1)
+    grad_gain_two = jnp.sum(
+        gate_weight.astype(F32) * gate_sum + up_weight.astype(F32) * up_sum, axis=1
+    )
+    return (
+        mixed_out,
+        grad_tokens.astype(BF16),
+        rows_of(grad_keys),
+        rows_of(grad_values),
+        gain_one * q_sum,
+        o_sum.astype(F32),
+        gain_two * gate_sum,
+        gain_two * up_sum,
+        down_sum.T,
+        grad_gain_one,
+        grad_gain_two,
+    )
+
+
+def to_slices(weight, nh):
+    rows, cols = weight.shape
+    parts = weight.reshape(rows, nh, cols // nh).swapaxes(0, 1)
+    return lax.all_to_all(parts, "head", 0, 0, tiled=False).reshape(nh * rows, cols // nh)
+
+
+def from_slices(part, nh):
+    rows, cols = part.shape
+    parts = part.reshape(nh, rows // nh, cols)
+    parts = lax.all_to_all(parts, "head", 0, 0, tiled=False)
+    return parts.swapaxes(0, 1).reshape(rows // nh, nh * cols)
+
+
+def gather_head(part):
+    return lax.all_gather(part, "head", axis=0, tiled=True)
+
+
+def scatter_head(full):
+    return lax.psum_scatter(full.astype(BF16), "head", scatter_dimension=0, tiled=True)
+
+
+def per_device_plain(
+    nh,
+    ns,
+    tokens,
+    keys,
+    values,
+    q_weight,
+    o_weight,
+    gate_weight,
+    up_weight,
+    down_weight,
+    attn_gain,
+    ffn_gain,
+    span_order,
+    doc_lengths,
+    cotangent,
+):
+    local, width = tokens.shape
+    rows = q_weight.shape[0]
+
     def shuffle(field):
         return field.reshape(local, nh, ns, rows).swapaxes(1, 2).reshape(local, width)
 
@@ -279,9 +975,11 @@
 
 def solution(mesh):
     both = ("head", "seq")
+    nh, ns = mesh.shape["head"], mesh.shape["seq"]
+    body = per_device if (nh, ns) == (NH, NS) else per_device_plain
     rows, cols, line, own = P(both, None), P(None, both), P(both), P("seq", None)
     return jax.shard_map(
-        functools.partial(per_device, mesh.shape["head"], mesh.shape["seq"]),
+        functools.partial(body, nh, ns),
         mesh=mesh,
         in_specs=(rows,) * 7 + (cols, line, line, own, own, rows),
         out_specs=(rows,) * 8 + (cols, line, line),

time: 926 us -> 647 us (0.70)
  waiting for transfers between devices: 600 us -> 77.7 us
  Pallas kernels: 21 us -> 403 us
  blocking collectives: 76 us -> 0 us
  matrix products: 86.3 us -> 56.4 us
  starting transfers between devices: 27.5 us -> 0.21 us
    pallas_call x1 -> x8, Pallas kernels: 7.55 us -> 391 us  [the longest x1 229 us: forward_call(): pl.pallas_call(forward_kernel, out_shape=out_shape, in_specs=[ANY] * 9 +...]
    all_gather x9 -> x0, waiting for transfers between devices: 281 us -> none  [the longest x5 151 us: gather_seq(): return lax.all_gather(part, 'seq', axis=0, tiled=True)]
    reduce_scatter x4 -> x0, waiting for transfers between devices: 157 us -> none  [scatter_head(): lax.psum_scatter(full.astype(BF16), 'head', scatter_dimension=0, tiled=True)]
    all_to_all x5 -> x0, blocking collectives: 76 us -> none  [the longest x4 59.6 us: to_slices(): lax.all_to_all(parts, 'head', 0, 0, tiled=False)]
    reduce_scatter x5, waiting for transfers between devices: 148 us -> 77.6 us  [scatter_seq(): lax.psum_scatter(full.astype(BF16), 'seq', scatter_dimension=0, tiled=True)]
    dot_general x15 -> x13, matrix products: 86.3 us -> 56.4 us  [dot(): lax.dot_general(left, right, (dims, ((), ())), preferred_element_type=F32)]
    all_to_all x7 -> x0, starting transfers between devices: 26.1 us -> none  [the longest x5 19.1 us: from_slices(): parts = lax.all_to_all(parts, 'head', 0, 0, tiled=False)]
    convert_element_type x16 -> x5, local copies, waits for them, and re-layouts: 24.3 us -> 9.28 us  [the longest x2 4.94 us: per_device(): up_sum = rows_of(up_sum).astype(F32)]
  transfers between devices with their start and end apart: 25 -> 5, of which waited for: 19 -> 3; matrix products, arithmetic and copies ran while one was open for 14% -> 9% of each run, Pallas kernels for 2% -> 17%
where the time goes in v2:
time: 647 us; the launch traced here: 636 us
  Pallas kernels  403 us (62%)
  waiting for transfers between devices  77.7 us (12%)
  local copies, waits for them, and re-layouts  63.2 us (10%)
  matrix products  56.4 us (9%)
  other arithmetic  20.6 us (3%)
  between operations  14.8 us (2%)
    pallas_call x1, Pallas kernels, forward_call(): pl.pallas_call(forward_kernel, out_shape=out_shape, in_specs=[ANY] * 9 +...  229 us
    pallas_call x3, Pallas kernels, rs_head(): pl.pallas_call(functools.partial(rs_kernel, nh), out_shape=jax.ShapeDtype...  87.2 us
    reduce_scatter x5, waiting for transfers between devices, scatter_seq(): lax.psum_scatter(full.astype(BF16), 'seq', scatter_dimension=0, tiled=True)  77.6 us
    dot_general x13, matrix products, dot(): lax.dot_general(left, right, (dims, ((), ())), preferred_element_type=F32)  56.4 us
    pallas_call x3, Pallas kernels, a2a_head(): pl.pallas_call(functools.partial(a2a_kernel, nh, m), out_shape=[jax.Shape...  51.7 us
    pallas_call x1, Pallas kernels, ag_head(): pl.pallas_call(functools.partial(ag_kernel, nh), out_shape=jax.ShapeDtype...  23.3 us
  transfers between devices with their start and end apart: 5, of which 3 were waited for; matrix products, arithmetic and copies ran while one was open for 9% of the time, Pallas kernels for 17%

profile of v2, /device:TPU:0, one launch (start us, length us, event | category | flops | bytes accessed | tf_op | source)
XLA Modules:
  0.0 636.5 jit_solution(871917560765753408)
XLA Ops:
  10.6 2.5 fusion.3
  13.1 1.4 reshape.276
  14.5 2.5 reshape.277
  17.0 2.5 reshape.275
  25.7 1.5 copy_bitcast_fusion
  27.2 228.6 %forward.1 = (bf16[8,4,64,256]{3,2,1,0:T(8,128)(2,1)}, bf16[8,4,64,688]{3,2,1,0:T(8,128)(2,1)}, bf16[8,4,64,688]{3,2,1,0:T(8,128)(2,1)}, bf16[8,4,64,688]{3,2,1,...) custom-call(bf16[8,64,256]{2,1,0:T(8,128)(2,1)} %bitcast.129, ...), custom_call_target="tpu_custom_call" | custom-call | tf_op jit(solution)/shard_map/forward/pallas_call | solution.py:697
  255.8 6.4 %fusion.26 = f32[1024,688]{0,1:T(8,128)S(1)} fusion(bf16[1024,2048]{1,0:T(8,128)(2,1)} %bitcast.146, bf16[2048,688]{1,0:T(8,128)(2,1)} %bitcast.156), kind=kOutput, calls=%fused_computation.78 | convolution fusion | flops 2885681152 | bytes 9830400 | tf_op jit(solution)/shard_map/dot_general | solution.py:23
  262.3 3.6 multiply_convert_fusion.2
  265.9 4.5 convolution_convert_fusion.4
  270.4 4.2 multiply_convert_fusion
  274.6 4.5 convolution_convert_fusion.3
  279.1 5.9 fusion.27
  285.0 4.5 convolution_convert_fusion.2
  289.5 5.9 add_convert_fusion
  295.4 29.3 %sum_ffn.1 = f32[128,2048]{1,0:T(8,128)S(1)} custom-call(bf16[8,128,2048]{2,1,0:T(8,128)(2,1)S(1)} %bitcast.104), custom_call_target="tpu_custom_call" | custom-call | tf_op jit(solution)/shard_map/sum_ffn/pallas_call | solution.py:270
  326.9 23.3 %gather_dh.1 = bf16[8,128,2048]{2,1,0:T(8,128)(2,1)} custom-call(bf16[128,2048]{1,0:T(8,128)(2,1)} %fusion.25.x_ref), custom_call_target="tpu_custom_call" | custom-call | tf_op jit(solution)/shard_map/gather_dh/pallas_call | solution.py:217
  350.1 4.4 convolution_convert_fusion.5
  354.7 4.6 copy.116
  359.3 4.0 copy.117
  363.4 4.6 copy.118
  368.0 3.9 copy.119
  372.0 4.0 convolution_convert_fusion.7.do_ref
  376.0 12.8 %attend_back.1 = (bf16[1024,256]{1,0:T(8,128)(2,1)S(1)}, bf16[1024,256]{1,0:T(8,128)(2,1)S(1)}, bf16[1024,256]{1,0:T(8,128)(2,1)S(1)}) custom-call(bf16[1024,256]{1,0:T(8,128)(2,1)S(1)} %copy-done.7, bf16[1024,256]{1,0:T(8,128)(2,1)S(1)} %bitcast.108, bf16[1024,256]{1,0:T(8,128)(2,1)S(1)} %bitcast.109, ...), custom_call_target="tpu_custom_call" | custom-call | flops 2684354560 | bytes 4718592 | tf_op jit(solution)/shard_map/attend_back/pallas_call | solution.py:120
  388.9 1.4 convolution_convert_fusion.6
  391.4 4.8 copy.113
  396.2 3.9 copy.114
  400.1 15.4 %back_kv.1 = (bf16[8,128,256]{2,1,0:T(8,128)(2,1)}, bf16[8,128,256]{2,1,0:T(8,128)(2,1)}) custom-call(bf16[8,128,256]{2,1,0:T(8,128)(2,1)} %bitcast.106, bf16[8,128,256]{2,1,0:T(8,128)(2,1)} %bitcast.107), custom_call_target="tpu_custom_call" | custom-call | tf_op jit(solution)/shard_map/back_kv/pallas_call | solution.py:304
  415.4 2.0 copy.110
  417.5 2.0 copy.123
  419.5 2.0 copy.111
  421.6 2.0 copy.124
  423.6 5.8 convolution_convert_fusion.1
  429.5 29.1 %sum_mixed.1 = f32[128,2048]{1,0:T(8,128)S(1)} custom-call(bf16[8,128,2048]{2,1,0:T(8,128)(2,1)S(1)} %bitcast.105), custom_call_target="tpu_custom_call" | custom-call | tf_op jit(solution)/shard_map/sum_mixed/pallas_call | solution.py:270
  459.9 28.8 %sum_q.1 = f32[128,2048]{1,0:T(8,128)S(1)} custom-call(bf16[8,128,2048]{2,1,0:T(8,128)(2,1)S(1)} %bitcast.103), custom_call_target="tpu_custom_call" | custom-call | tf_op jit(solution)/shard_map/sum_q/pallas_call | solution.py:270
  490.4 1.8 convert_element_type.151
  492.2 13.1 %reduce-scatter.14.cloned.1.call-done = bf16[512,688]{1,0:T(8,128)(2,1)} async-done(((bf16[2048,688]{1,0:T(8,128)(2,1)}), bf16[512,688]{1,0:T(8,128)(2,1)}) %reduce-scatter.14.cloned.1.call-update) | async-done | bytes 704528 | tf_op jit(solution)/shard_map/reduce_scatter | solution.py:337
  505.2 21.0 %back_ffn.1 = (bf16[8,64,688]{2,1,0:T(8,128)(2,1)}, bf16[8,64,688]{2,1,0:T(8,128)(2,1)}) custom-call(bf16[8,64,688]{2,1,0:T(8,128)(2,1)} %bitcast.132, bf16[8,64,688]{2,1,0:T(8,128)(2,1)} %bitcast.133), custom_call_target="tpu_custom_call" | custom-call | tf_op jit(solution)/shard_map/back_ffn/pallas_call | solution.py:304
  527.5 2.1 copy.120
  529.5 2.2 reshape.313
  531.8 3.5 reduce-scatter.6.cloned.1.call-done
  535.3 61.1 %reduce-scatter.8.cloned.1.call-done = bf16[512,688]{1,0:T(8,128)(2,1)} async-done(((bf16[2048,688]{1,0:T(8,128)(2,1)}), bf16[512,688]{1,0:T(8,128)(2,1)}) %reduce-scatter.8.cloned.1.call-update) | async-done | bytes 704528 | tf_op jit(solution)/shard_map/reduce_scatter | solution.py:337
  596.4 15.3 %back_q.1 = (bf16[8,64,256]{2,1,0:T(8,128)(2,1)}, bf16[8,64,688]{2,1,0:T(8,128)(2,1)}) custom-call(bf16[8,64,256]{2,1,0:T(8,128)(2,1)} %bitcast.138, bf16[8,64,688]{2,1,0:T(8,128)(2,1)} %bitcast.134), custom_call_target="tpu_custom_call" | custom-call | tf_op jit(solution)/shard_map/back_q/pallas_call | solution.py:304
  613.0 2.1 copy.121
  615.0 2.9 reshape.314
  619.2 2.1 copy.122
  621.3 3.0 reshape.315
  624.3 2.6 fusion.14
  626.9 2.6 fusion.2
  (107 shorter events, 19.9 us)
Async XLA Ops:
  7.2 483.2 %reduce-scatter.10.cloned.1.call-start = ((), (), s32[]{:S(2)}) async-start(), calls=%async_computation.7 | async-start | bytes 1310720 | tf_op jit(solution)/shard_map/reduce_scatter | solution.py:337
  13.1 7.4 %copy-start.9 = (bf16[128,2048]{1,0:T(8,128)(2,1)S(1)}, bf16[128,2048]{1,0:T(8,128)(2,1)}, u32[]{:S(2)}) copy-start(bf16[128,2048]{1,0:T(8,128)(2,1)} %tokens.1) | copy-start | bytes 1572868
  14.5 7.2 %copy-start.27 = (bf16[64]{0:T(256)(128)(2,1)S(1)}, bf16[64]{0:T(256)(128)(2,1)}, u32[]{:S(2)}) copy-start(bf16[64]{0:T(256)(128)(2,1)} %param.21) | copy-start | bytes 388
  14.5 7.2 %copy-start.16 = (bf16[64,2048]{1,0:T(8,128)(2,1)S(1)}, bf16[64,2048]{1,0:T(8,128)(2,1)}, u32[]{:S(2)}) copy-start(bf16[64,2048]{1,0:T(8,128)(2,1)} %param.16) | copy-start | bytes 786436
  20.5 2.0 copy-start.17
  21.8 2.0 copy-start.18
  255.8 6.4 %copy-start.21 = (bf16[8,128,2048]{2,1,0:T(8,128)(2,1)S(1)}, bf16[8,128,2048]{2,1,0:T(8,128)(2,1)}, u32[]{:S(2)}) copy-start(bf16[8,128,2048]{2,1,0:T(8,128)(2,1)} %get-tuple-element.42) | copy-start | bytes 12582916
  255.8 6.4 %copy-start.24 = (bf16[8,4,64,688]{3,2,1,0:T(8,128)(2,1)S(1)}, bf16[8,4,64,688]{3,2,1,0:T(8,128)(2,1)}, u32[]{:S(2)}) copy-start(bf16[8,4,64,688]{3,2,1,0:T(8,128)(2,1)} %get-tuple-element.44) | copy-start | bytes 8454148
  262.3 3.6 copy-start.22
  265.9 4.6 copy-start.28
  265.9 4.5 copy-start.23
  274.6 4.5 copy-start.25
  295.4 29.3 %copy-start.8 = (f32[128,2048]{1,0:T(8,128)S(1)}, f32[128,2048]{1,0:T(8,128)}, u32[]{:S(2)}) copy-start(f32[128,2048]{1,0:T(8,128)} %get-tuple-element.41) | copy-start | bytes 3145732
  324.7 1.0 copy-start.12
  326.8 23.3 %copy-start.26 = (bf16[1024,256]{1,0:T(8,128)(2,1)S(1)}, bf16[1024,256]{1,0:T(8,128)(2,1)}, u32[]{:S(2)}) copy-start(bf16[1024,256]{1,0:T(8,128)(2,1)} %get-tuple-element.65) | copy-start | bytes 1572868
  354.6 137.6 %reduce-scatter.12.cloned.1.call-start = ((), (), s32[]{:S(2)}) async-start(), calls=%async_computation.8 | async-start | bytes 3932160 | tf_op jit(solution)/shard_map/reduce_scatter | solution.py:337
  363.3 141.9 %reduce-scatter.14.cloned.1.call-start = ((), (), s32[]{:S(2)}) async-start(), calls=%async_computation.9 | async-start | bytes 3932160 | tf_op jit(solution)/shard_map/reduce_scatter | solution.py:337
  371.9 163.4 %reduce-scatter.6.cloned.1.call-start = ((), (), s32[]{:S(2)}) async-start(), calls=%async_computation.5 | async-start | bytes 1310720 | tf_op jit(solution)/shard_map/reduce_scatter | solution.py:337
  371.9 4.0 copy-start
  371.9 4.0 copy-start.3
  372.0 4.0 copy-start.4
  372.0 4.0 copy-start.5
  372.0 4.0 copy-start.6
  372.0 4.0 copy-start.7
  376.0 12.8 %copy-start.20 = (bf16[8,128,2048]{2,1,0:T(8,128)(2,1)S(1)}, bf16[8,128,2048]{2,1,0:T(8,128)(2,1)}, u32[]{:S(2)}) copy-start(bf16[8,128,2048]{2,1,0:T(8,128)(2,1)} %get-tuple-element.55) | copy-start | bytes 12582916
  388.8 1.4 copy-start.1
  388.8 1.4 copy-start.2
  391.3 205.0 %reduce-scatter.8.cloned.1.call-start = ((), (), s32[]{:S(2)}) async-start(), calls=%async_computation.6 | async-start | bytes 3932160 | tf_op jit(solution)/shard_map/reduce_scatter | solution.py:337
  429.4 29.1 %copy-start.15 = (bf16[8,4,64,256]{3,2,1,0:T(8,128)(2,1)S(1)}, bf16[8,4,64,256]{3,2,1,0:T(8,128)(2,1)}, u32[]{:S(2)}) copy-start(bf16[8,4,64,256]{3,2,1,0:T(8,128)(2,1)} %get-tuple-element.57) | copy-start | bytes 3145732
  459.9 28.8 %copy-start.10 = (bf16[128,2048]{1,0:T(8,128)(2,1)S(1)}, bf16[128,2048]{1,0:T(8,128)(2,1)}, u32[]{:S(2)}) copy-start(bf16[128,2048]{1,0:T(8,128)(2,1)} %tokens.1) | copy-start | bytes 1572868
  619.2 5.1 copy-start.19
  621.3 5.6 copy-start.11
  624.2 2.7 copy-start.13
  624.2 2.7 copy-start.14
Sparse Core Ops, SparseCore 0:
  354.7 26.3 reduce-scatter.9
  383.6 58.8 reduce-scatter.11
  444.9 60.2 reduce-scatter.13
  508.1 27.1 reduce-scatter.5
  537.4 58.8 reduce-scatter.7

commit v3 on v1

--- a/solution.py
+++ b/solution.py
@@ -9,6 +9,7 @@
 from jax.sharding import PartitionSpec as P
 
 HEAD_DIM = 128
+NH, NS = 8, 4
 EPS = 1e-06
 BF16 = jnp.bfloat16
 F32 = jnp.float32
@@ -141,6 +142,1098 @@
     )(query, keys, values, grad, lse, place_q, place_k)
 
 
+MESH = pl.DeviceIdType.MESH
+ANY = pl.BlockSpec(memory_space=pl.ANY)
+VMEM = pl.BlockSpec(memory_space=pltpu.VMEM)
+SMEM = pl.BlockSpec(memory_space=pltpu.SMEM)
+
+
+def slices_of(weight, nh):
+    rows, cols = weight.shape
+    return weight.reshape(rows, nh, cols // nh).swapaxes(0, 1)
+
+
+def rows_of(parts):
+    nh, rows, cols = parts.shape
+    return parts.swapaxes(0, 1).reshape(rows, nh * cols)
+
+
+def flat(parts):
+    return parts.reshape(parts.shape[0] * parts.shape[1], parts.shape[2])
+
+
+def remote(src, dst, send, recv, to):
+    return pltpu.make_async_remote_copy(
+        src_ref=src, dst_ref=dst, send_sem=send, recv_sem=recv, device_id=to, device_id_type=MESH
+    )
+
+
+class Net:
+    def __init__(self):
+        self.h = lax.axis_index("head")
+        self.s = lax.axis_index("seq")
+        self.open = []
+
+    def peer(self, k):
+        return (lax.bitwise_xor(self.h, k), self.s)
+
+    def greet(self):
+        barrier = pltpu.get_barrier_semaphore()
+        for k in range(1, NH):
+            pl.semaphore_signal(barrier, inc=1, device_id=self.peer(k), device_id_type=MESH)
+        for k in range(1, NS):
+            there = (self.h, lax.rem(self.s + k, NS))
+            pl.semaphore_signal(barrier, inc=1, device_id=there, device_id_type=MESH)
+        pl.semaphore_wait(barrier, NH - 1 + NS - 1)
+
+    def put(self, src, dst, send, recv, to):
+        copy = remote(src, dst, send, recv, to)
+        copy.start()
+        self.open.append(copy)
+        return copy
+
+    def swap(self, src, dst, send, recv, own):
+        mine = pltpu.make_async_copy(src(self.h), dst(self.h), own)
+        mine.start()
+        copies = []
+        for k in (6, 2, 4, 1, 5, 3, 7):
+            to = self.peer(k)
+            copy = remote(src(to[0]), dst(self.h), send.at[k - 1], recv.at[k - 1], to)
+            copy.start()
+            copies.append(copy)
+
+        def finish():
+            for copy in copies:
+                copy.wait()
+            mine.wait()
+
+        return finish
+
+    def gather(self, src, dst, send, recv, own):
+        half = src.shape[0] // 2
+        lo, hi = pl.ds(0, half), pl.ds(half, half)
+        h, core, px, py = self.h, self.peer(1), self.peer(2), self.peer(4)
+        x, y, d = px[0], py[0], lax.bitwise_xor(h, 6)
+        mine = pltpu.make_async_copy(src, dst.at[h], own)
+        mine.start()
+
+        def put(i, a, b, to):
+            return self.put(a, b, send.at[i], recv.at[i], to)
+
+        xa = put(0, src.at[lo], dst.at[h, lo], px)
+        yb = put(1, src.at[hi], dst.at[h, hi], py)
+        c0 = put(2, src, dst.at[h], core)
+        xb = put(3, src.at[hi], dst.at[h, hi], px)
+        ya = put(4, src.at[lo], dst.at[h, lo], py)
+
+        def finish():
+            near = [c0]
+            xa.wait_recv()
+            fy = put(5, dst.at[x, lo], dst.at[x, lo], py)
+            near.append(put(6, dst.at[x, lo], dst.at[x, lo], core))
+            yb.wait_recv()
+            fx = put(7, dst.at[y, hi], dst.at[y, hi], px)
+            near.append(put(8, dst.at[y, hi], dst.at[y, hi], core))
+            xb.wait_recv()
+            near.append(put(9, dst.at[x, hi], dst.at[x, hi], core))
+            ya.wait_recv()
+            near.append(put(10, dst.at[y, lo], dst.at[y, lo], core))
+            fy.wait_recv()
+            near.append(put(11, dst.at[d, lo], dst.at[d, lo], core))
+            fx.wait_recv()
+            near.append(put(12, dst.at[d, hi], dst.at[d, hi], core))
+            for copy in near:
+                copy.wait_recv()
+            mine.wait()
+
+        return finish
+
+    def scatter(self, source, block, core_in, held, far_in, send, recv):
+        core = self.peer(1)
+        order = (6, 2, 4, 0)
+
+        def put(i, a, b, to):
+            copy = remote(a, b, send.at[i], recv.at[i], to)
+            copy.start()
+            return copy
+
+        near = [
+            put(i, source(i, lax.bitwise_xor(core[0], k)), core_in.at[i], core)
+            for i, k in enumerate(order)
+        ]
+        far = []
+        for i, k in enumerate(order):
+            value = block(i, lax.bitwise_xor(self.h, k))
+            near[i].wait_recv()
+            value = value + core_in[i].astype(F32)
+            if k:
+                held[i] = value.astype(BF16)
+                far.append(put(4 + i, held.at[i], far_in.at[i], self.peer(k)))
+
+        def finish():
+            result = value
+            for i in (1, 2, 0):
+                far[i].wait_recv()
+                result = result + far_in[i].astype(F32)
+            for copy in near + far:
+                copy.wait_send()
+            return result
+
+        return finish
+
+    def z_gather(self, src, block, send, recv):
+        s = self.s
+        steps = (2, -2, 1, -1)
+
+        def there(d):
+            return (self.h, s + d)
+
+        def copy(n):
+            return remote(src, block(s), send.at[n], recv.at[s], there(steps[n]))
+
+        def valid(d):
+            return (s + d >= 0) & (s + d < NS)
+
+        middle = (s == 1) | (s == 2)
+        origin = jnp.where(s == 2, 0, NS - 1)
+        target = (self.h, NS - 1 - origin)
+
+        def relay():
+            return remote(block(origin), block(origin), send.at[4], recv.at[origin], target)
+
+        for n, d in enumerate(steps):
+
+            @pl.when(valid(d))
+            def _():
+                copy(n).start()
+
+        def forward():
+            @pl.when(middle)
+            def _():
+                relay().wait_recv()
+                relay().start()
+
+        def finish():
+            for t in range(NS):
+                waited = ((s == 2) & (t == 0)) | ((s == 1) & (t == NS - 1))
+
+                @pl.when((s != t) & jnp.logical_not(waited))
+                def _():
+                    remote(block(t), block(t), send.at[0], recv.at[t], (self.h, s)).wait_recv()
+
+        def drain():
+            for n, d in enumerate(steps):
+
+                @pl.when(valid(d))
+                def _():
+                    copy(n).wait_send()
+
+            @pl.when(middle)
+            def _():
+                relay().wait_send()
+
+        return forward, finish, drain
+
+    def close(self):
+        for copy in self.open:
+            copy.wait_send()
+
+
+def fetch(pairs, sems):
+    copies = [pltpu.make_async_copy(a, b, sems.at[i]) for i, (a, b) in enumerate(pairs)]
+    for copy in copies:
+        copy.start()
+    for copy in copies:
+        copy.wait()
+
+
+def z_scatter(net, block, got, comb, send, recv):
+    s = net.s
+    first, last = s == 0, s == NS - 1
+    middle = (s == 1) | (s == 2)
+    far = jnp.where(s == 1, NS - 1, 0)
+    inner = jnp.where(first, 1, NS - 2)
+
+    def joined(src):
+        return remote(src, got.at[s], send.at[0], recv.at[s], (net.h, far))
+
+    def to_join():
+        return remote(block(NS - 1 - s), comb, send.at[0], recv.at[NS], (net.h, inner))
+
+    def direct(n, d):
+        return remote(block(s + d), got.at[s], send.at[n], recv.at[s], (net.h, s + d))
+
+    steps = ((1, 2, first), (2, -2, last), (3, 1, s < NS - 1), (4, -1, s > 0))
+
+    def start_join():
+        @pl.when(first | last)
+        def _():
+            to_join().start()
+
+    def start():
+        for n, d, where in steps:
+
+            @pl.when(where)
+            def _():
+                direct(n, d).start()
+
+    def join(one, two, sems):
+        @pl.when(middle)
+        def _():
+            to_join().wait_recv()
+            fetch([(comb, one), (block(far), two)], sems)
+            one[...] = (one[...].astype(F32) + two[...].astype(F32)).astype(BF16)
+            joined(one).start()
+
+    def finish(total, bufs, sems):
+        mine = pltpu.make_async_copy(block(s), bufs.at[NS], sems.at[NS])
+        mine.start()
+
+        def comes(t):
+            return (s != t) & (s + t != NS - 1) if t in (0, NS - 1) else (s != t)
+
+        for t in range(NS):
+
+            @pl.when(comes(t))
+            def _():
+                remote(got.at[t], got.at[t], send.at[0], recv.at[t], (net.h, s)).wait_recv()
+                pltpu.make_async_copy(got.at[t], bufs.at[t], sems.at[t]).start()
+
+        mine.wait()
+        total[...] = bufs[NS].astype(F32)
+        for t in range(NS):
+
+            @pl.when(comes(t))
+            def _():
+                pltpu.make_async_copy(got.at[t], bufs.at[t], sems.at[t]).wait()
+                total[...] += bufs[t].astype(F32)
+
+    def drain():
+        @pl.when(first | last)
+        def _():
+            to_join().wait_send()
+
+        for n, d, where in steps:
+
+            @pl.when(where)
+            def _():
+                direct(n, d).wait_send()
+
+        @pl.when(middle)
+        def _():
+            joined(comb).wait_send()
+
+    return start_join, start, join, finish, drain
+
+
+def make_places(order, lengths, place_q, place_k):
+    group, count = place_q.shape[0], order.shape[1]
+    width = group // count
+    for shape, dim in (((group, 1), 0), ((1, group), 1)):
+        slots = lax.broadcasted_iota(jnp.int32, shape, dim)
+        position = slots
+        for c in range(count):
+            inside = (slots >= c * width) & (slots < (c + 1) * width)
+            position = jnp.where(inside, slots + (order[0, c] - c) * width, position)
+        segment = jnp.zeros(shape, jnp.int32)
+        bound = 0
+        for j in range(lengths.shape[1]):
+            bound = bound + lengths[0, j]
+            segment = segment + (position >= bound).astype(jnp.int32)
+        if dim == 0:
+            place_q[:, 0:1] = position
+            place_q[:, 1:2] = segment
+        else:
+            place_k[0:1, :] = position
+            place_k[1:2, :] = segment
+
+
+def mask(place_q, place_k, rows):
+    return (place_q[rows, 1:2] == place_k[1:2, :]) & (place_k[0:1, :] <= place_q[rows, 0:1])
+
+
+def lane_block(w, p, wide):
+    return w.at[:, pl.ds(pl.multiple_of(p * wide, wide), wide)]
+
+
+def load(pairs, sems, base):
+    copies = [pltpu.make_async_copy(a, b, sems.at[base + i]) for i, (a, b) in enumerate(pairs)]
+    for copy in copies:
+        copy.start()
+
+    def finish():
+        for copy in copies:
+            copy.wait()
+
+    return finish
+
+
+def forward_kernel(
+    q_weight,
+    gate_weight,
+    up_weight,
+    down_rows,
+    gain_one,
+    gain_two,
+    tokens,
+    o_own,
+    keys,
+    values,
+    cot_own,
+    order,
+    lengths,
+    w_q,
+    w_o,
+    w_gate,
+    w_up,
+    w_down,
+    n1_all,
+    k_all,
+    v_all,
+    cot_all,
+    n2_all,
+    got_down,
+    comb_down,
+    spread,
+    query,
+    attended,
+    lse,
+    hidden_out,
+    mixed_out,
+    gate_term,
+    up_term,
+    down_sum,
+    q_own,
+    place_q,
+    place_k,
+    wq_v,
+    wo_v,
+    wg_v,
+    wu_v,
+    wd_v,
+    norm_v,
+    cot_v,
+    k_v,
+    v_v,
+    n1_own,
+    n2_own,
+    near_out,
+    core_in,
+    held,
+    far_in,
+    act_v,
+    grad_gate,
+    grad_up,
+    down_term,
+    join_v,
+    bufs,
+    total,
+    swap_send,
+    swap_recv,
+    ag_send,
+    ag_recv,
+    rs_send,
+    rs_recv,
+    z_send,
+    z_recv,
+    own,
+    load_sem,
+):
+    net = Net()
+    s = net.s
+    local, width = tokens.shape
+    group = NH * local
+    wide, hid = query.shape[1], act_v.shape[1]
+    step = 256
+    tiles = group // step
+    net.greet()
+    gate_own, up_own, down_own = (bufs.at[i] for i in range(3))
+
+    def swap(j, src, dst):
+        return net.swap(src, dst, swap_send.at[j], swap_recv.at[j], own.at[j])
+
+    def gather(j, src, dst):
+        return net.gather(src, dst, ag_send.at[j], ag_recv.at[j], own.at[8 + j])
+
+    def z_gather(j, src, block):
+        return net.z_gather(src, block, z_send.at[j], z_recv.at[j])
+
+    def slab(w):
+        return lambda t: w.at[:, t]
+
+    def slices(weight, gain, out):
+        field = weight[...]
+        if gain is not None:
+            field = (field.astype(F32) * gain[...]).astype(BF16)
+        cols = out.shape[2]
+        for p in range(NH):
+            out[p] = field[:, p * cols : (p + 1) * cols]
+
+    zo = z_gather(0, o_own, lambda t: w_o.at[t])
+    mine = pltpu.make_async_copy(o_own, w_o.at[s], own.at[15])
+    mine.start()
+    slices(q_weight, gain_one, q_own)
+    q_there = swap(0, lambda p: q_own.at[p], lambda p: w_q.at[p, s])
+    slices(gate_weight, gain_two, gate_own)
+    gate_there = swap(1, lambda p: gate_own.at[p], lambda p: w_gate.at[p, s])
+    inputs = tokens[...].astype(F32)
+    n1_own[...] = (inputs * rms_scale(inputs)).astype(BF16)
+    n1_there = gather(0, n1_own, n1_all)
+    q_there()
+    zq = z_gather(1, w_q.at[:, s], slab(w_q))
+    slices(up_weight, gain_two, up_own)
+    k_there = swap(2, lambda p: lane_block(keys, p, wide), lambda p: k_all.at[p])
+    v_there = swap(3, lambda p: lane_block(values, p, wide), lambda p: v_all.at[p])
+    gate_there()
+    zg = z_gather(2, w_gate.at[:, s], slab(w_gate))
+    up_there = swap(4, lambda p: up_own.at[p], lambda p: w_up.at[p, s])
+    slices(down_rows, None, down_own)
+    make_places(order, lengths, place_q, place_k)
+    n1_there()
+    zo[0]()
+    zq[0]()
+    down_there = swap(5, lambda p: down_own.at[p], lambda p: w_down.at[p, s])
+    cot_there = gather(2, cot_own, cot_all)
+    n1_here = load([(n1_all, norm_v)], load_sem, 0)
+    up_there()
+    zu = z_gather(3, w_up.at[:, s], slab(w_up))
+    k_there()
+    v_there()
+    kv_here = load([(k_all, k_v), (v_all, v_v)], load_sem, 1)
+    zq[1]()
+    wq_here = load([(w_q, wq_v)], load_sem, 3)
+    down_there()
+    zd = z_gather(4, w_down.at[:, s], slab(w_down))
+    n1_here()
+    wq_here()
+
+    @pl.loop(0, tiles)
+    def _(i):
+        rows = pl.ds(pl.multiple_of(i * step, step), step)
+        part = norm_v[pl.ds(i * (step // local), step // local)].reshape(step, width)
+        query[rows, :] = dot(part, wq_v[...].reshape(width, wide), ((1,), (0,))).astype(BF16)
+
+    cot_there()
+    cot_here = load([(cot_all, cot_v)], load_sem, 0)
+    kv_here()
+    zo[1]()
+    mine.wait()
+    wo_here = load([(w_o, wo_v)], load_sem, 3)
+
+    scale = 1.0 / math.sqrt(HEAD_DIM)
+    for head in range(wide // HEAD_DIM):
+        cols = slice(head * HEAD_DIM, (head + 1) * HEAD_DIM)
+
+        @pl.loop(0, tiles)
+        def _(i):
+            rows = pl.ds(pl.multiple_of(i * step, step), step)
+            raw = dot(query[rows, cols], k_v[:, :, cols].reshape(group, HEAD_DIM), ((1,), (1,)))
+            logits = jnp.where(mask(place_q, place_k, rows), raw * scale, -1e30)
+            top = jnp.max(logits, axis=-1, keepdims=True)
+            expo = jnp.exp(logits - top)
+            norm = jnp.sum(expo, axis=-1, keepdims=True)
+            probs = (expo * (1.0 / norm)).astype(BF16)
+            attended[rows, cols] = dot(
+                probs, v_v[:, :, cols].reshape(group, HEAD_DIM), ((1,), (0,))
+            ).astype(BF16)
+            lse[rows, cols] = jnp.broadcast_to(top + jnp.log(norm), (step, HEAD_DIM))
+
+    wo_here()
+
+    def o_block(i, p):
+        rows = pl.ds(pl.multiple_of(p * local, local), local)
+        return dot(attended[rows, :], wo_v[...].reshape(wide, width), ((1,), (0,)))
+
+    def o_near(i, p):
+        near_out[i] = o_block(i, p).astype(BF16)
+        return near_out.at[i]
+
+    o_sum = net.scatter(o_near, o_block, core_in, held, far_in, rs_send.at[0], rs_recv.at[0])
+    cot_here()
+    hidden = inputs + o_sum()
+    hidden_out[...] = hidden
+    n2_own[...] = (hidden * rms_scale(hidden)).astype(BF16)
+    n2_there = gather(1, n2_own, n2_all)
+    zg[0]()
+    n2_there()
+    n2_here = load([(n2_all, norm_v)], load_sem, 0)
+    zg[1]()
+    wg_here = load([(w_gate, wg_v)], load_sem, 1)
+    zu[0]()
+    zu[1]()
+    wu_here = load([(w_up, wu_v)], load_sem, 2)
+    n2_here()
+    wg_here()
+    wu_here()
+
+    def matrix(w):
+        return w[...].reshape(width, hid)
+
+    @pl.loop(0, tiles)
+    def _(i):
+        rows = pl.ds(pl.multiple_of(i * step, step), step)
+        part = norm_v[pl.ds(i * (step // local), step // local)].reshape(step, width)
+        gate = dot(part, matrix(wg_v), ((1,), (0,)))
+        up = dot(part, matrix(wu_v), ((1,), (0,)))
+        sigma = jax.nn.sigmoid(gate)
+        silu = gate * sigma
+        act_v[rows, :] = (silu * up).astype(BF16)
+        grad_gate[rows, :] = (up * sigma * (1.0 + gate * (1.0 - sigma))).astype(BF16)
+        grad_up[rows, :] = silu.astype(BF16)
+
+    fold = width // NH
+
+    def columns(field, i):
+        cols = pl.ds(pl.multiple_of(i * fold, fold), fold)
+        return field[:, :, cols].reshape(group, fold)
+
+    def term(left, right):
+        return dot(left, right, ((0,), (0,))).astype(BF16).reshape(NS, fold // NS, hid)
+
+    @pl.loop(0, NH)
+    def _(i):
+        down_term[i] = term(columns(cot_v, i), act_v[...])
+
+    z_down = z_scatter(
+        net, lambda t: down_term.at[:, t], got_down, comb_down, z_send.at[5], z_recv.at[5]
+    )
+    z_down[0]()
+    z_down[1]()
+    zd[0]()
+    zd[1]()
+    load([(w_down, wd_v)], load_sem, 3)()
+
+    @pl.loop(0, tiles)
+    def _(i):
+        rows = pl.ds(pl.multiple_of(i * step, step), step)
+        part = cot_v[pl.ds(i * (step // local), step // local)].reshape(step, width)
+        grad_act = dot(part, matrix(wd_v), ((1,), (0,)))
+        grad_gate[rows, :] = (grad_act * grad_gate[rows, :].astype(F32)).astype(BF16)
+        grad_up[rows, :] = (grad_act * grad_up[rows, :].astype(F32)).astype(BF16)
+
+    def mixed_block(i, p):
+        rows = pl.ds(pl.multiple_of(p * local, local), local)
+        return dot(act_v[rows, :], matrix(wd_v), ((1,), (1,)))
+
+    def mixed_near(i, p):
+        near_out[i] = mixed_block(i, p).astype(BF16)
+        return near_out.at[i]
+
+    mixed_sum = net.scatter(
+        mixed_near, mixed_block, core_in, held, far_in, rs_send.at[1], rs_recv.at[1]
+    )
+    z_down[2](join_v, bufs.at[NS], load_sem)
+
+    @pl.loop(0, NH)
+    def _(i):
+        part = columns(norm_v, i)
+        gate_term[i] = term(part, grad_gate[...])
+        up_term[i] = term(part, grad_up[...])
+
+    @pl.loop(0, tiles)
+    def _(i):
+        rows = pl.ds(pl.multiple_of(i * step, step), step)
+        part = dot(grad_gate[rows, :], matrix(wg_v), ((1,), (1,)))
+        part = part + dot(grad_up[rows, :], matrix(wu_v), ((1,), (1,)))
+        norm_v[pl.ds(i * (step // local), step // local)] = part.astype(BF16).reshape(
+            step // local, local, width
+        )
+
+    spread_there = load([(norm_v, spread)], load_sem, 5)
+    mixed_out[...] = (hidden_out[...] + mixed_sum()).astype(BF16)
+    z_down[3](total, bufs, load_sem)
+    down_sum[...] = total[...].astype(BF16)
+    spread_there()
+    for z in (zo, zq, zg, zu, zd):
+        z[2]()
+    z_down[4]()
+    net.close()
+
+
+def forward_call(q_weight, gate_weight, up_weight, down_rows, gain_one, gain_two, tokens, o_own, keys, values, cot_own, order, lengths):
+    local, width = tokens.shape
+    group = NH * local
+    rows = o_own.shape[0]
+    wide, hid = width // NH, gate_weight.shape[1] // NH
+
+    def bf(*shape):
+        return jax.ShapeDtypeStruct(shape, BF16)
+
+    out_shape = [
+        bf(NH, NS, rows, wide),
+        bf(NS, rows, width),
+        bf(NH, NS, rows, hid),
+        bf(NH, NS, rows, hid),
+        bf(NH, NS, rows, hid),
+        bf(NH, local, width),
+        bf(NH, local, wide),
+        bf(NH, local, wide),
+        bf(NH, local, width),
+        bf(NH, local, width),
+        bf(NS, NH, rows, hid),
+        bf(NH, rows, hid),
+        bf(NH, local, width),
+        bf(group, wide),
+        bf(group, wide),
+        jax.ShapeDtypeStruct((group, wide), F32),
+        jax.ShapeDtypeStruct((local, width), F32),
+        bf(local, width),
+        bf(NH, NS, rows, hid),
+        bf(NH, NS, rows, hid),
+        bf(NH, rows, hid),
+    ]
+    dma = pltpu.SemaphoreType.DMA
+    vm = pltpu.VMEM
+    return pl.pallas_call(
+        forward_kernel,
+        out_shape=out_shape,
+        in_specs=[VMEM] * 7 + [ANY] * 4 + [SMEM] * 2,
+        out_specs=[ANY] * 13 + [VMEM] * 8,
+        scratch_shapes=[
+            vm((NH, rows, wide), BF16),
+            vm((group, 2), jnp.int32),
+            vm((2, group), jnp.int32),
+            vm((NH, NS, rows, wide), BF16),
+            vm((NS, rows, width), BF16),
+            vm((NH, NS, rows, hid), BF16),
+            vm((NH, NS, rows, hid), BF16),
+            vm((NH, NS, rows, hid), BF16),
+            vm((NH, local, width), BF16),
+            vm((NH, local, width), BF16),
+            vm((NH, local, wide), BF16),
+            vm((NH, local, wide), BF16),
+            vm((local, width), BF16),
+            vm((local, width), BF16),
+            vm((4, local, width), BF16),
+            vm((4, local, width), BF16),
+            vm((3, local, width), BF16),
+            vm((3, local, width), BF16),
+            vm((group, hid), BF16),
+            vm((group, hid), BF16),
+            vm((group, hid), BF16),
+            vm((NH, NS, rows, hid), BF16),
+            vm((NH, rows, hid), BF16),
+            vm((NS + 1, NH, rows, hid), BF16),
+            vm((NH, rows, hid), F32),
+            dma((6, 7)),
+            dma((6, 7)),
+            dma((3, 13)),
+            dma((3, 13)),
+            dma((2, 7)),
+            dma((2, 7)),
+            dma((6, 5)),
+            dma((6, NS + 1)),
+            dma((16,)),
+            dma((8,)),
+        ],
+        compiler_params=pltpu.CompilerParams(
+            collective_id=0, has_side_effects=True, vmem_limit_bytes=63 << 20
+        ),
+        name="forward",
+    )(q_weight, gate_weight, up_weight, down_rows, gain_one, gain_two, tokens, o_own, keys, values, cot_own, order, lengths)
+
+
+def backward_kernel(
+    tokens,
+    cot_own,
+    hidden_in,
+    gate_term,
+    up_term,
+    spread,
+    down_sum,
+    w_o,
+    w_q,
+    n1_all,
+    query,
+    k_all,
+    v_all,
+    attended,
+    lse,
+    order,
+    lengths,
+    d_tokens,
+    o_out,
+    d_keys,
+    d_values,
+    q_out,
+    gate_out,
+    up_out,
+    down_out,
+    got_ffn,
+    comb_ffn,
+    got_q,
+    comb_q,
+    got_o,
+    comb_o,
+    place_q,
+    place_k,
+    own_v,
+    near_out,
+    core_in,
+    held,
+    far_in,
+    dh_v,
+    dh_own,
+    dh_all,
+    n1_v,
+    wo_v,
+    wq_v,
+    q_v,
+    k_v,
+    v_v,
+    att_v,
+    lse_v,
+    da_v,
+    dq_v,
+    dk_v,
+    dv_v,
+    dk_sum,
+    dv_sum,
+    q_term,
+    o_term,
+    joins,
+    q_join,
+    o_join,
+    bufs,
+    q_bufs,
+    o_bufs,
+    total,
+    results,
+    q_total,
+    q_result,
+    o_total,
+    z_send,
+    z_recv,
+    swap_send,
+    swap_recv,
+    ag_send,
+    ag_recv,
+    rs_send,
+    rs_recv,
+    own,
+    load_sem,
+):
+    net = Net()
+    h, s = net.h, net.s
+    local, width = tokens.shape
+    group = NH * local
+    wide = query.shape[1]
+    step = 256
+    tiles = group // step
+    scale = 1.0 / math.sqrt(HEAD_DIM)
+    net.greet()
+
+    def swap(j, src, dst):
+        return net.swap(src, dst, swap_send.at[j], swap_recv.at[j], own.at[j])
+
+    def scatter(j, source, block):
+        return net.scatter(
+            source, block, core_in.at[j], held.at[j], far_in.at[j], rs_send.at[j], rs_recv.at[j]
+        )
+
+    def z_sum(j, block, got, comb):
+        z = z_scatter(net, block, got, comb, z_send.at[j], z_recv.at[j])
+        z[0]()
+        z[1]()
+        return z
+
+    z_gate = z_sum(0, lambda t: gate_term.at[:, t], got_ffn.at[0], comb_ffn.at[0])
+    z_up = z_sum(1, lambda t: up_term.at[:, t], got_ffn.at[1], comb_ffn.at[1])
+    own_here = [
+        load([(spread.at[lax.bitwise_xor(h, k)], own_v.at[i])], load_sem, i)
+        for i, k in enumerate((6, 2, 4, 0))
+    ]
+
+    def spread_block(i, p):
+        own_here[i]()
+        return own_v[i].astype(F32)
+
+    ffn_sum = scatter(0, lambda i, p: spread.at[p], spread_block)
+    backs = [swap(2, lambda p: down_sum.at[p], lambda p: down_out.at[p])]
+    here = load(
+        [
+            (w_o, wo_v),
+            (w_q, wq_v),
+            (query, q_v),
+            (k_all, k_v),
+            (v_all, v_v),
+            (attended, att_v),
+            (lse, lse_v),
+            (n1_all, n1_v),
+        ],
+        load_sem,
+        8,
+    )
+    make_places(order, lengths, place_q, place_k)
+    hidden = hidden_in[...]
+    scale_two = rms_scale(hidden)
+    normed_two = hidden * scale_two
+    here()
+    scaled_two = ffn_sum()
+    grad_hidden = cot_own[...].astype(F32) + scale_two * (
+        scaled_two - normed_two * jnp.mean(scaled_two * normed_two, axis=-1, keepdims=True)
+    )
+    dh_v[...] = grad_hidden
+    dh_own[...] = grad_hidden.astype(BF16)
+    dh_there = net.gather(dh_own, dh_all, ag_send, ag_recv, own.at[8])
+    z_gate[2](joins.at[0], bufs.at[NS], load_sem)
+    dh_there()
+
+    @pl.loop(0, tiles)
+    def _(i):
+        rows = pl.ds(pl.multiple_of(i * step, step), step)
+        part = dh_all[pl.ds(i * (step // local), step // local)].reshape(step, width)
+        da_v[rows, :] = dot(part, wo_v[...].reshape(wide, width), ((1,), (1,))).astype(BF16)
+
+    for head in range(wide // HEAD_DIM):
+        cols = slice(head * HEAD_DIM, (head + 1) * HEAD_DIM)
+        dk_sum[...] = jnp.zeros_like(dk_sum)
+        dv_sum[...] = jnp.zeros_like(dv_sum)
+
+        @pl.loop(0, tiles)
+        def _(i):
+            rows = pl.ds(pl.multiple_of(i * step, step), step)
+            keys = k_v[:, :, cols].reshape(group, HEAD_DIM)
+            part, grad = q_v[rows, cols], da_v[rows, cols]
+            raw = dot(part, keys, ((1,), (1,)))
+            logits = jnp.where(mask(place_q, place_k, rows), raw * scale, -1e30)
+            probs = jnp.exp(logits - lse_v[rows, cols][:, :1])
+            grad_probs = dot(grad, v_v[:, :, cols].reshape(group, HEAD_DIM), ((1,), (1,)))
+            inner = jnp.sum(probs * grad_probs, axis=-1, keepdims=True)
+            grad_raw = (probs * (grad_probs - inner) * scale).astype(BF16)
+            dq_v[rows, cols] = dot(grad_raw, keys, ((1,), (0,))).astype(BF16)
+            dk_sum[...] += dot(grad_raw, part, ((0,), (0,)))
+            dv_sum[...] += dot(probs.astype(BF16), grad, ((0,), (0,)))
+
+        dk_v[:, :, cols] = dk_sum[...].astype(BF16).reshape(NH, local, HEAD_DIM)
+        dv_v[:, :, cols] = dv_sum[...].astype(BF16).reshape(NH, local, HEAD_DIM)
+
+    z_up[2](joins.at[1], bufs.at[NS], load_sem)
+
+    def q_block(i, p):
+        rows = pl.ds(pl.multiple_of(p * local, local), local)
+        return dot(dq_v[rows, :], wq_v[...].reshape(width, wide), ((1,), (1,)))
+
+    def q_near(i, p):
+        near_out[i] = q_block(i, p).astype(BF16)
+        return near_out.at[i]
+
+    q_sum = scatter(1, q_near, q_block)
+    fold = width // NH
+
+    @pl.loop(0, NH)
+    def _(i):
+        cols = pl.ds(pl.multiple_of(i * fold, fold), fold)
+        part = dot(n1_v[:, :, cols].reshape(group, fold), dq_v[...], ((0,), (0,)))
+        q_term[i] = part.astype(BF16).reshape(NS, fold // NS, wide)
+
+    zq = z_sum(2, lambda t: q_term.at[:, t], got_q, comb_q)
+
+    @pl.loop(0, NH)
+    def _(i):
+        cols = pl.ds(pl.multiple_of(i * fold, fold), fold)
+        part = dot(att_v[...], dh_all[:, :, cols].reshape(group, fold), ((0,), (0,)))
+        o_term[:, :, cols] = part.astype(BF16).reshape(NS, wide // NS, fold)
+
+    zo = z_sum(3, lambda t: o_term.at[t], got_o, comb_o)
+    backs.append(swap(0, lambda p: dk_v.at[p], lambda p: lane_block(d_keys, p, wide)))
+    backs.append(swap(1, lambda p: dv_v.at[p], lambda p: lane_block(d_values, p, wide)))
+    z_gate[3](total, bufs, load_sem)
+    results[0] = total[...].astype(BF16)
+    backs.append(swap(3, lambda p: results.at[0, p], lambda p: gate_out.at[p]))
+
+    inputs = tokens[...].astype(F32)
+    scale_one = rms_scale(inputs)
+    normed_one = inputs * scale_one
+    scaled_one = q_sum()
+    d_tokens[...] = (
+        dh_v[...]
+        + scale_one
+        * (scaled_one - normed_one * jnp.mean(scaled_one * normed_one, axis=-1, keepdims=True))
+    ).astype(BF16)
+    zq[2](q_join, q_bufs.at[NS], load_sem)
+    zo[2](o_join, o_bufs.at[NS], load_sem)
+    z_up[3](total, bufs, load_sem)
+    results[1] = total[...].astype(BF16)
+    backs.append(swap(4, lambda p: results.at[1, p], lambda p: up_out.at[p]))
+    zq[3](q_total, q_bufs, load_sem)
+    q_result[...] = q_total[...].astype(BF16)
+    backs.append(swap(5, lambda p: q_result.at[p], lambda p: lane_block(q_out, p, wide)))
+    zo[3](o_total, o_bufs, load_sem)
+    o_out[...] = o_total[...]
+    for back in backs:
+        back()
+    for z in (z_gate, z_up, zq, zo):
+        z[4]()
+    net.close()
+
+
+def backward_call(tokens, cot_own, hidden, gate_term, up_term, spread, down_sum, w_o, w_q, n1_all, query, k_all, v_all, attended, lse, order, lengths):
+    local, width = tokens.shape
+    group = NH * local
+    rows, wide, hid = w_q.shape[2], w_q.shape[3], gate_term.shape[3]
+
+    def bf(*shape):
+        return jax.ShapeDtypeStruct(shape, BF16)
+
+    out_shape = [
+        bf(local, width),
+        jax.ShapeDtypeStruct((rows, width), F32),
+        bf(local, width),
+        bf(local, width),
+        bf(rows, width),
+        bf(NH, rows, hid),
+        bf(NH, rows, hid),
+        bf(NH, rows, hid),
+        bf(2, NS, NH, rows, hid),
+        bf(2, NH, rows, hid),
+        bf(NS, NH, rows, wide),
+        bf(NH, rows, wide),
+        bf(NS, rows, width),
+        bf(rows, width),
+    ]
+    dma = pltpu.SemaphoreType.DMA
+    vm = pltpu.VMEM
+    return pl.pallas_call(
+        backward_kernel,
+        out_shape=out_shape,
+        in_specs=[VMEM] * 3 + [ANY] * 12 + [SMEM] * 2,
+        out_specs=[VMEM] * 2 + [ANY] * 12,
+        scratch_shapes=[
+            vm((group, 2), jnp.int32),
+            vm((2, group), jnp.int32),
+            vm((4, local, width), BF16),
+            vm((4, local, width), BF16),
+            vm((2, 4, local, width), BF16),
+            vm((2, 3, local, width), BF16),
+            vm((2, 3, local, width), BF16),
+            vm((local, width), F32),
+            vm((local, width), BF16),
+            vm((NH, local, width), BF16),
+            vm((NH, local, width), BF16),
+            vm((NS, rows, width), BF16),
+            vm((NH, NS, rows, wide), BF16),
+            vm((group, wide), BF16),
+            vm((NH, local, wide), BF16),
+            vm((NH, local, wide), BF16),
+            vm((group, wide), BF16),
+            vm((group, wide), F32),
+            vm((group, wide), BF16),
+            vm((group, wide), BF16),
+            vm((NH, local, wide), BF16),
+            vm((NH, local, wide), BF16),
+            vm((group, HEAD_DIM), F32),
+            vm((group, HEAD_DIM), F32),
+            vm((NH, NS, rows, wide), BF16),
+            vm((NS, rows, width), BF16),
+            vm((2, NH, rows, hid), BF16),
+            vm((NH, rows, wide), BF16),
+            vm((rows, width), BF16),
+            vm((NS + 1, NH, rows, hid), BF16),
+            vm((NS + 1, NH, rows, wide), BF16),
+            vm((NS + 1, rows, width), BF16),
+            vm((NH, rows, hid), F32),
+            vm((2, NH, rows, hid), BF16),
+            vm((NH, rows, wide), F32),
+            vm((NH, rows, wide), BF16),
+            vm((rows, width), F32),
+            dma((4, 5)),
+            dma((4, NS + 1)),
+            dma((6, 7)),
+            dma((6, 7)),
+            dma((13,)),
+            dma((13,)),
+            dma((2, 7)),
+            dma((2, 7)),
+            dma((9,)),
+            dma((16,)),
+        ],
+        compiler_params=pltpu.CompilerParams(
+            collective_id=1, has_side_effects=True, vmem_limit_bytes=62 << 20
+        ),
+        name="backward",
+    )(tokens, cot_own, hidden, gate_term, up_term, spread, down_sum, w_o, w_q, n1_all, query, k_all, v_all, attended, lse, order, lengths)
+
+
+def per_device(
+    nh,
+    ns,
+    tokens,
+    keys,
+    values,
+    q_weight,
+    o_weight,
+    gate_weight,
+    up_weight,
+    down_weight,
+    attn_gain,
+    ffn_gain,
+    span_order,
+    doc_lengths,
+    cotangent,
+):
+    gain_one = attn_gain.astype(F32)[:, None]
+    gain_two = ffn_gain.astype(F32)[:, None]
+    (
+        w_q, w_o, _, _, _, n1_all, k_all, v_all, _, _, _, _, spread,
+        query, attended, lse, hidden, mixed_out, gate_term, up_term, down_sum,
+    ) = forward_call(
+        q_weight,
+        gate_weight,
+        up_weight,
+        down_weight.T,
+        gain_one,
+        gain_two,
+        tokens,
+        o_weight,
+        keys,
+        values,
+        cotangent,
+        span_order,
+        doc_lengths,
+    )
+    grad_tokens, o_sum, grad_keys, grad_values, q_sum, gate_sum, up_sum, down_sum = backward_call(
+        tokens,
+        cotangent,
+        hidden,
+        gate_term,
+        up_term,
+        spread,
+        down_sum,
+        w_o,
+        w_q,
+        n1_all,
+        query,
+        k_all,
+        v_all,
+        attended,
+        lse,
+        span_order,
+        doc_lengths,
+    )[:8]
+    q_sum = q_sum.astype(F32)
+    gate_sum = rows_of(gate_sum).astype(F32)
+    up_sum = rows_of(up_sum).astype(F32)
+    down_sum = rows_of(down_sum).astype(F32)
+    grad_gain_one = jnp.sum(q_weight.astype(F32) * q_sum, axis=1)
+    grad_gain_two = jnp.sum(
+        gate_weight.astype(F32) * gate_sum + up_weight.astype(F32) * up_sum, axis=1
+    )
+    return (
+        mixed_out,
+        grad_tokens,
+        grad_keys,
+        grad_values,
+        gain_one * q_sum,
+        o_sum,
+        gain_two * gate_sum,
+        gain_two * up_sum,
+        down_sum.T,
+        grad_gain_one,
+        grad_gain_two,
+    )
+
+
 def to_slices(weight, nh):
     rows, cols = weight.shape
     parts = weight.reshape(rows, nh, cols // nh).swapaxes(0, 1)
@@ -170,7 +1263,7 @@
     return lax.psum_scatter(full.astype(BF16), "head", scatter_dimension=0, tiled=True)
 
 
-def per_device(
+def per_device_plain(
     nh,
     ns,
     tokens,
@@ -279,9 +1372,11 @@
 
 def solution(mesh):
     both = ("head", "seq")
+    nh, ns = mesh.shape["head"], mesh.shape["seq"]
+    body = per_device if (nh, ns) == (NH, NS) else per_device_plain
     rows, cols, line, own = P(both, None), P(None, both), P(both), P("seq", None)
     return jax.shard_map(
-        functools.partial(per_device, mesh.shape["head"], mesh.shape["seq"]),
+        functools.partial(body, nh, ns),
         mesh=mesh,
         in_specs=(rows,) * 7 + (cols, line, line, own, own, rows),
         out_specs=(rows,) * 8 + (cols, line, line),

time: 926 us -> 449 us (0.48)
  waiting for transfers between devices: 600 us -> 0 us
  Pallas kernels: 21 us -> 418 us
  matrix products: 86.3 us -> 0 us
  blocking collectives: 76 us -> 0 us
  local copies, waits for them, and re-layouts: 62.8 us -> 13.3 us
  starting transfers between devices: 27.5 us -> 0 us
  other arithmetic: 26.8 us -> 8.59 us
  between operations: 15.3 us -> 1.19 us
    pallas_call x2, Pallas kernels: 21 us -> 418 us  [the longest x1 271 us: forward_call(): pl.pallas_call(forward_kernel, out_shape=out_shape, in_specs=[VMEM] * 7 +...]
    reduce_scatter x9 -> x0, waiting for transfers between devices: 306 us -> none  [the longest x4 157 us: scatter_head(): lax.psum_scatter(full.astype(BF16), 'head', scatter_dimension=0, tiled=True)]
    all_gather x9 -> x0, waiting for transfers between devices: 281 us -> none  [the longest x5 151 us: gather_seq(): return lax.all_gather(part, 'seq', axis=0, tiled=True)]
    dot_general x15 -> x0, matrix products: 86.3 us -> none  [dot(): lax.dot_general(left, right, (dims, ((), ())), preferred_element_type=F32)]
    all_to_all x5 -> x0, blocking collectives: 76 us -> none  [the longest x4 59.6 us: to_slices(): lax.all_to_all(parts, 'head', 0, 0, tiled=False)]
    all_to_all x7 -> x0, starting transfers between devices: 26.1 us -> none  [the longest x5 19.1 us: from_slices(): parts = lax.all_to_all(parts, 'head', 0, 0, tiled=False)]
    convert_element_type x16 -> x4, local copies, waits for them, and re-layouts: 24.3 us -> 5.25 us  [the longest x2 2.62 us: per_device(): gate_sum = rows_of(gate_sum).astype(F32)]
    reshape x10 -> x0, local copies, waits for them, and re-layouts: 17.8 us -> none  [the longest x8 15.1 us: to_slices(): parts = weight.reshape(rows, nh, cols // nh).swapaxes(0, 1)]
  transfers between devices with their start and end apart: 25 -> 0, of which waited for: 19 -> 0; matrix products, arithmetic and copies ran while one was open for 14% -> 0% of each run, Pallas kernels for 2% -> 0%
where the time goes in v3:
time: 449 us; the launch traced here: 441 us
  Pallas kernels  418 us (93%)
  local copies, waits for them, and re-layouts  13.3 us (3%)
  other arithmetic  8.59 us (2%)
    pallas_call x1, Pallas kernels, forward_call(): pl.pallas_call(forward_kernel, out_shape=out_shape, in_specs=[VMEM] * 7 +...  271 us
    pallas_call x1, Pallas kernels, backward_call(): pl.pallas_call(backward_kernel, out_shape=out_shape, in_specs=[VMEM] * 3...  146 us

profile of v3, /device:TPU:0, one launch (start us, length us, event | category | flops | bytes accessed | tf_op | source)
XLA Modules:
  0.0 440.6 jit_solution(17022364672873788989)
XLA Ops:
  0.6 0.7 fusion.2
  1.3 0.7 fusion.1
  2.0 0.7 copy.27.gain_two
  2.7 0.7 copy.26.gain_one
  3.4 271.5 %forward.1 = (bf16[8,4,64,256]{3,2,1,0:T(8,128)(2,1)}, bf16[4,64,2048]{2,1,0:T(8,128)(2,1)}, bf16[8,4,64,688]{3,2,1,0:T(8,128)(2,1)}, bf16[8,4,64,688]{3,2,1,0:T...) custom-call(bf16[64,2048]{1,0:T(8,128)(2,1)} %q_weight.1, ...), custom_call_target="tpu_custom_call" | custom-call | tf_op jit(solution)/shard_map/forward/pallas_call | solution.py:787
  274.9 0.0 copy-start.1
  274.9 146.0 %backward.1 = (bf16[128,2048]{1,0:T(8,128)(2,1)}, f32[64,2048]{1,0:T(8,128)}, bf16[128,2048]{1,0:T(8,128)(2,1)}, bf16[128,2048]{1,0:T(8,128)(2,1)}, bf16[64,2048...) custom-call(bf16[128,2048]{1,0:T(8,128)(2,1)} %tokens.3, ...), custom_call_target="tpu_custom_call" | custom-call | tf_op jit(solution)/shard_map/backward/pallas_call | solution.py:1097
  420.9 0.0 copy-start.4
  420.9 0.0 copy-done.1
  420.9 2.5 fusion
  423.5 0.0 copy-done.4
  423.5 0.1 convert_bitcast_fusion.2
  423.6 0.9 copy.28
  424.6 0.0 copy-start.2
  424.6 0.0 copy-start.3
  424.6 1.7 reshape.33
  426.3 0.0 copy-done.2
  426.3 0.0 copy-done.3
  426.3 0.2 convert_bitcast_fusion
  426.5 0.9 copy.30
  427.4 1.7 reshape.35
  429.1 0.9 copy.29
  430.1 0.0 copy-start
  430.1 1.7 reshape.34
  431.8 0.0 copy-done
  431.8 0.0 copy-start.5
  431.8 0.0 copy-start.9
  431.8 4.4 add_reduce_fusion
  436.2 0.0 copy-start.8
  436.2 0.0 copy-done.5
  436.2 0.0 copy-start.7
  436.2 0.8 copy.36
  437.0 0.0 copy-done.9
  437.0 0.0 copy-start.6
  437.0 0.8 copy.37
  437.8 0.0 copy-done.8
  437.8 0.8 copy.38
  438.6 0.0 copy-done.7
  438.6 0.8 copy.39
  439.4 0.0 copy-done.6
  439.4 0.8 copy.40
Async XLA Ops:
  274.9 146.1 %copy-start.1 = (bf16[64,2048]{1,0:T(8,128)(2,1)S(1)}, bf16[64,2048]{1,0:T(8,128)(2,1)}, u32[]{:S(2)}) copy-start(bf16[64,2048]{1,0:T(8,128)(2,1)} %q_weight.1) | copy-start | bytes 786436
  420.9 2.6 copy-start.4
  424.6 1.7 copy-start.2
  424.6 1.7 copy-start.3
  430.1 1.7 copy-start
  431.8 4.4 copy-start.5
  431.8 5.2 %copy-start.9 = (bf16[128,2048]{1,0:T(8,128)(2,1)S(1)}, bf16[128,2048]{1,0:T(8,128)(2,1)}, u32[]{:S(2)}) copy-start(bf16[128,2048]{1,0:T(8,128)(2,1)} %get-tuple-element.78) | copy-start | bytes 1572868
  436.2 1.6 copy-start.8
  436.2 2.4 copy-start.7
  437.0 2.4 copy-start.6
